TPU v7x, 128 devices: a whole 4x4x4 slice. The times are simulated.
128 devices in a mesh: dev: 128 (over y, x, z, core).
Axes of the slice: x: 4, y: 4, z: 4, core: 2. Of those that a mesh axis runs over, the one named last changes fastest.
Arguments:
- emb_a: float32 [131072, 128], P('dev'), may hold values from -6 to 6
- emb_b: float32 [131072, 128], P('dev'), may hold values from -6 to 6
- cat_a: int32 [131072], P('dev'), may hold values from 0 to 15
- cat_b: int32 [131072], P('dev'), may hold values from 0 to 15
- mass_a: float32 [131072], P('dev'), may hold values from 0.5 to 2
- mass_b: float32 [131072], P('dev'), may hold values from 0.5 to 2
- pair_list: int32 [128, 7], P('dev'), may hold values from 0 to 127, as said below
- pair_count: int32 [128], P('dev'), may hold values from 1 to 7, as said below
Outputs:
- mapped_a: float32 [131072, 128], P('dev')
- mapped_b: float32 [131072, 128], P('dev')
Inputs may be any that keep to these rules, and one draw needn't show every extreme that they name: `pair_list`: row p lists, in rising order in its first pair_count[p] entries, distinct B slabs within 3 slabs of p, always including p itself; its other entries equal p. Some row lists all 7 slabs around it. pair_count[p] is the number of slabs listed in row p of pair_list; some row has 7.
All inputs are finite; a program needn't handle non-finite values.
Results may differ from a plain program's by a relative error of at most 0.0003.
Values sent between devices are 32-bit elements; how exact they have to be, the bound alone decides.
No kernel may reach another device: no remote copies, remote signals or barrier semaphores. Data moves between devices by JAX's collectives and lax.ppermute only.
A program may use at most 128 MiB of HBM per device.

v0:
```python
from functools import partial

import jax
import jax.numpy as jnp
from jax import lax
from jax.sharding import PartitionSpec as P

SPAN = 3
SLOTS = 7
ITERS = 2


penalty = 0.5
epsilon = 0.1
highest = lax.Precision.HIGHEST


def shifted(block, axis, distance):
    devices = range(lax.axis_size(axis))
    route = [(i - distance, i) for i in devices if i - distance in devices]
    return lax.ppermute(block, axis, route)


def unit_rows(matrix):
    return matrix * lax.rsqrt(jnp.sum(matrix * matrix, axis=1, keepdims=True) + 1e-06)


def kernel_block(left_unit, left_cat, right_unit, right_cat):
    inner = lax.dot_general(
        left_unit,
        right_unit,
        (((1,), (1,)), ((), ())),
        precision=highest,
        preferred_element_type=jnp.float32,
    )
    mismatch = (left_cat[:, None] != right_cat[None, :]).astype(jnp.float32)
    distance = 1.0 - inner + penalty * mismatch
    return jnp.exp(-distance / epsilon)


def column_apply(scale_part, kernel):
    return jnp.dot(kernel, scale_part, precision=highest, preferred_element_type=jnp.float32)


def row_apply(scale_part, kernel):
    return jnp.dot(scale_part, kernel, precision=highest, preferred_element_type=jnp.float32)


def both_maps(column_part, raw_part, scaled_a, row_part, kernel):
    num_a = jnp.dot(
        kernel,
        column_part[:, None] * raw_part,
        precision=highest,
        preferred_element_type=jnp.float32,
    )
    den_a = jnp.dot(kernel, column_part, precision=highest, preferred_element_type=jnp.float32)
    num_b = lax.dot_general(
        kernel,
        scaled_a,
        (((0,), (0,)), ((), ())),
        precision=highest,
        preferred_element_type=jnp.float32,
    )
    den_b = jnp.dot(row_part, kernel, precision=highest, preferred_element_type=jnp.float32)
    return (num_a, den_a, num_b, den_b)


def shards(emb_a, emb_b, cat_a, cat_b, mass_a, mass_b, pair_list, pair_count):
    position = lax.axis_index("dev")
    slab_rows = emb_a.shape[0]
    width = emb_a.shape[1]
    offsets = list(range(-SPAN, SPAN + 1))
    usable = jnp.arange(SLOTS) < pair_count[0]
    active = {}
    for offset in offsets:
        active[offset] = jnp.any((pair_list[0] == position + offset) & usable).astype(jnp.float32)
    cats_b = cat_b.astype(jnp.float32)
    cats_a = cat_a.astype(jnp.float32)
    fetched = {0: (emb_b, cats_b)}
    for offset in offsets:
        if offset != 0:
            fetched[offset] = shifted((emb_b, cats_b), "dev", -offset)
    unit_a = unit_rows(emb_a)
    unit_near = {}
    for offset in offsets:
        unit_near[offset] = unit_rows(fetched[offset][0])

    def with_kernel(offset, consume):
        kernel = (
            kernel_block(unit_a, cats_a, unit_near[offset], fetched[offset][1]) * active[offset]
        )
        return consume(kernel)

    def near_scales(col_scale):
        near = {0: col_scale}
        for offset in offsets:
            if offset != 0:
                near[offset] = shifted(col_scale, "dev", -offset)
        return near

    nothing_row = jnp.zeros((slab_rows,), jnp.float32)
    col_scale = jnp.ones((slab_rows,), jnp.float32)
    row_scale = jnp.ones((slab_rows,), jnp.float32)
    for iteration in range(ITERS):
        if iteration == 0:
            near = {}
            for offset in offsets:
                near[offset] = col_scale
        else:
            near = near_scales(col_scale)
        row_total = nothing_row
        for offset in offsets:
            row_total = row_total + with_kernel(offset, partial(column_apply, near[offset]))
        row_scale = mass_a / row_total
        partials = {}
        for offset in offsets:
            partials[offset] = with_kernel(offset, partial(row_apply, row_scale))
        summed = partials[0]
        for owner_offset in offsets:
            if owner_offset != 0:
                summed = summed + shifted(partials[owner_offset], "dev", owner_offset)
        col_scale = mass_b / summed
    near = near_scales(col_scale)
    scaled_a = row_scale[:, None] * emb_a
    num_a = jnp.zeros((slab_rows, width), jnp.float32)
    den_a = nothing_row
    backs = {}
    for offset in offsets:
        maps = with_kernel(
            offset, partial(both_maps, near[offset], fetched[offset][0], scaled_a, row_scale)
        )
        num_a = num_a + maps[0]
        den_a = den_a + maps[1]
        backs[offset] = (maps[2], maps[3])
    mapped_a = num_a / den_a[:, None]
    back_num = backs[0][0]
    back_den = backs[0][1]
    for offset in offsets:
        if offset != 0:
            arrived = shifted((backs[offset][0], backs[offset][1]), "dev", offset)
            back_num = back_num + arrived[0]
            back_den = back_den + arrived[1]
    mapped_b = back_num / back_den[:, None]
    return (mapped_a, mapped_b)


def solution(mesh):
    placed = (
        P("dev", None),
        P("dev", None),
        P("dev"),
        P("dev"),
        P("dev"),
        P("dev"),
        P("dev", None),
        P("dev"),
    )
    return jax.shard_map(
        shards,
        mesh=mesh,
        in_specs=placed,
        out_specs=(P("dev", None), P("dev", None)),
        check_vma=False,
    )
```

profile of v0, /device:TPU:25, one launch (start us, length us, event | category | flops | bytes accessed | tf_op | source)
XLA Modules:
  0.0 433.3 jit_solution(5554257441375061712)
XLA Ops:
  1.3 8.6 %collective-permute-start.11 = (f32[1024]{0:T(1024)S(1)}, f32[1024]{0:T(1024)S(1)}, u32[]{:S(2)}, u32[]{:S(2)}) collective-permute-start(f32[1024]{0:T(1024)S(1)} %convert_element_type.19), channel_id=1, source_target_pairs={{3,0},{4,1},{5,2},{6,3},{7,4},{8,5},{9,6},{10,7},{11,8},{12,9},{13... | collective-permute-start | bytes 12296 | tf_op jit(solution)/shard_map/ppermute | solution.py:21
  14.2 5.0 %collective-permute-start = (f32[1024,128]{1,0:T(8,128)}, f32[1024,128]{1,0:T(8,128)S(1)}, u32[]{:S(2)}, u32[]{:S(2)}) collective-permute-start(f32[1024,128]{1,0:T(8,128)} %param.9), channel_id=1, source_target_pairs={{0,3},{1,4},{2,5},{3,6},{4,7},{5,8},{6,9},{7,10},{8,11},{9,12},{10... | collective-permute-start | bytes 1572872 | tf_op jit(solution)/shard_map/ppermute | solution.py:21
  19.2 4.7 %collective-permute-start.10 = (f32[1024,128]{1,0:T(8,128)}, f32[1024,128]{1,0:T(8,128)S(1)}, u32[]{:S(2)}, u32[]{:S(2)}) collective-permute-start(f32[1024,128]{1,0:T(8,128)} %param.9), channel_id=1, source_target_pairs={{3,0},{4,1},{5,2},{6,3},{7,4},{8,5},{9,6},{10,7},{11,8},{12,9},{13... | collective-permute-start | bytes 1572872 | tf_op jit(solution)/shard_map/ppermute | solution.py:21
  33.7 5.7 %exponential_multiply_fusion.3 = f32[1024,1024]{1,0:T(8,128)S(1)} fusion(f32[]{:T(128)S(6)} %convert_element_type.23, f32[1024]{0:T(1024)S(1)} %convert_element_type.19, f32[1024]{0:T(1024)S(1)} %convert_element_type.18, f32[1024,128]{1,0:T(8,128)} %param.9, f32[1024,128]{1,0:T(8,128)} %param.8, f32[1024]{0:T(1024)S(1)} %get-tuple-element.11, ...), kind=kOutput, calls=%fused_computation.3 | convolution fusion | flops 1618214912 | bytes 5259268 | tf_op jit(solution)/shard_map/dot_general | solution.py:29
  43.1 3.7 collective-permute-start.5
  51.3 4.5 %exponential_multiply_fusion = f32[1024,1024]{1,0:T(8,128)S(1)} fusion(f32[]{:T(128)S(6)} %convert_element_type.26, f32[1024]{0:T(1024)S(1)} %collective-permute-done.11, f32[1024]{0:T(1024)S(1)} %convert_element_type.18, f32[1024,128]{1,0:T(8,128)S(1)} %collective-permute-done.10, f32[1024,128]{1,0:T(8,128)S(1)} %copy-done, f32[1024]{0:T(1024)S(1)} %add_rsqrt_fusion, ...), kind=kOutput, calls=%fused_computation | convolution fusion | flops 1618214912 | bytes 5259268 | tf_op jit(solution)/shard_map/dot_general | solution.py:29
  59.4 8.9 %collective-permute-done.2 = f32[1024,128]{1,0:T(8,128)S(1)} collective-permute-done((f32[1024,128]{1,0:T(8,128)S(1)}, f32[1024,128]{1,0:T(8,128)S(1)}, u32[]{:S(2)}, u32[]{:S(2)}) %collective-permute-start.2) | collective-permute-done | bytes 524320 | tf_op jit(solution)/shard_map/ppermute | solution.py:21
  70.5 7.0 %collective-permute-done.1 = f32[1024]{0:T(1024)S(1)} collective-permute-done((f32[1024]{0:T(1024)S(1)}, f32[1024]{0:T(1024)S(1)}, u32[]{:S(2)}, u32[]{:S(2)}) %collective-permute-start.1) | collective-permute-done | bytes 4128 | tf_op jit(solution)/shard_map/ppermute | solution.py:21
  79.8 4.5 %exponential_multiply_fusion.6 = f32[1024,1024]{1,0:T(8,128)S(1)} fusion(f32[]{:T(128)S(6)} %convert_element_type.20, f32[1024]{0:T(1024)S(1)} %collective-permute-done.1, f32[1024]{0:T(1024)S(1)} %convert_element_type.18, f32[1024,128]{1,0:T(8,128)S(1)} %collective-permute-done, f32[1024,128]{1,0:T(8,128)S(1)} %copy-done, f32[1024]{0:T(1024)S(1)} %add_rsqrt_fusion.6, ...), kind=kOutput, calls=%fused_computation.6 | convolution fusion | flops 1618214912 | bytes 5259268 | tf_op jit(solution)/shard_map/dot_general | solution.py:29
  88.0 9.1 %collective-permute-start.8 = (f32[1024,128]{1,0:T(8,128)S(1)}, f32[1024,128]{1,0:T(8,128)S(1)}, u32[]{:S(2)}, u32[]{:S(2)}) collective-permute-start(f32[1024,128]{1,0:T(8,128)S(1)} %copy-done.1), channel_id=1, source_target_pairs={{2,0},{3,1},{4,2},{5,3},{6,4},{7,5},{8,6},{9,7},{10,8},{11,9},{12,... | collective-permute-start | bytes 1572872 | tf_op jit(solution)/shard_map/ppermute | solution.py:21
  99.4 4.5 %exponential_multiply_fusion.5 = f32[1024,1024]{1,0:T(8,128)S(1)} fusion(f32[]{:T(128)S(6)} %convert_element_type.21, f32[1024]{0:T(1024)S(1)} %collective-permute-done.3, f32[1024]{0:T(1024)S(1)} %convert_element_type.18, f32[1024,128]{1,0:T(8,128)S(1)} %collective-permute-done.2, f32[1024,128]{1,0:T(8,128)S(1)} %copy-done, f32[1024]{0:T(1024)S(1)} %add_rsqrt_fusion.5, ...), kind=kOutput, calls=%fused_computation.5 | convolution fusion | flops 1618214912 | bytes 5259268 | tf_op jit(solution)/shard_map/dot_general | solution.py:29
  110.0 4.5 %exponential_multiply_fusion.4 = f32[1024,1024]{1,0:T(8,128)S(1)} fusion(f32[]{:T(128)S(6)} %convert_element_type.22, f32[1024]{0:T(1024)S(1)} %collective-permute-done.5, f32[1024]{0:T(1024)S(1)} %convert_element_type.18, f32[1024,128]{1,0:T(8,128)S(1)} %collective-permute-done.4, f32[1024,128]{1,0:T(8,128)S(1)} %copy-done, f32[1024]{0:T(1024)S(1)} %add_rsqrt_fusion.4, ...), kind=kOutput, calls=%fused_computation.4 | convolution fusion | flops 1618214912 | bytes 5259268 | tf_op jit(solution)/shard_map/dot_general | solution.py:29
  114.6 4.7 %exponential_multiply_fusion.2 = f32[1024,1024]{1,0:T(8,128)S(1)} fusion(f32[]{:T(128)S(6)} %convert_element_type.24, f32[1024]{0:T(1024)S(1)} %collective-permute-done.7, f32[1024]{0:T(1024)S(1)} %convert_element_type.18, f32[1024,128]{1,0:T(8,128)S(1)} %collective-permute-done.6, f32[1024,128]{1,0:T(8,128)S(1)} %copy-done, f32[1024]{0:T(1024)S(1)} %add_rsqrt_fusion.2, ...), kind=kOutput, calls=%fused_computation.2 | convolution fusion | flops 1618214912 | bytes 5259268 | tf_op jit(solution)/shard_map/dot_general | solution.py:29
  126.8 4.9 %exponential_multiply_fusion.1 = f32[1024,1024]{1,0:T(8,128)S(1)} fusion(f32[]{:T(128)S(6)} %convert_element_type.25, f32[1024]{0:T(1024)S(1)} %collective-permute-done.9, f32[1024]{0:T(1024)S(1)} %convert_element_type.18, f32[1024,128]{1,0:T(8,128)S(1)} %collective-permute-done.8, f32[1024,128]{1,0:T(8,128)S(1)} %copy-done, f32[1024]{0:T(1024)S(1)} %add_rsqrt_fusion.1, ...), kind=kOutput, calls=%fused_computation.1 | convolution fusion | flops 1618214912 | bytes 5259268 | tf_op jit(solution)/shard_map/dot_general | solution.py:29
  150.1 11.5 %collective-permute-start.13 = (f32[1024]{0:T(1024)S(1)}, f32[1024]{0:T(1024)S(1)}, u32[]{:S(2)}, u32[]{:S(2)}) collective-permute-start(f32[1024]{0:T(1024)S(1)} %bitcast.228), channel_id=1, source_target_pairs={{2,0},{3,1},{4,2},{5,3},{6,4},{7,5},{8,6},{9,7},{10,8},{11,9},{12,... | collective-permute-start | bytes 12296 | tf_op jit(solution)/shard_map/ppermute | solution.py:21
  214.9 4.1 fusion.115
  233.2 6.9 %fusion.30 = f32[1024,128]{1,0:T(8,128)S(1)} fusion(f32[1024,1024]{1,0:T(8,128)S(1)} %exponential_multiply_fusion, f32[1024,128]{1,0:T(8,128)S(1)} %copy-done, f32[1024]{0:T(1024)S(1)} %add_divide_fusion), kind=kOutput, calls=%fused_computation.48 | convolution fusion | flops 1610743808 | bytes 5246976 | tf_op jit(solution)/shard_map/dot_general | solution.py:57
  240.1 7.1 %fusion.32 = f32[1024,128]{1,0:T(8,128)S(1)} fusion(f32[1024,1024]{1,0:T(8,128)S(1)} %exponential_multiply_fusion.1, f32[1024,128]{1,0:T(8,128)S(1)} %copy-done, f32[1024]{0:T(1024)S(1)} %add_divide_fusion), kind=kOutput, calls=%fused_computation.50 | convolution fusion | flops 1610743808 | bytes 5246976 | tf_op jit(solution)/shard_map/dot_general | solution.py:57
  247.3 6.9 %fusion.36 = f32[1024,128]{1,0:T(8,128)S(1)} fusion(f32[1024,1024]{1,0:T(8,128)S(1)} %exponential_multiply_fusion.4, f32[1024,128]{1,0:T(8,128)S(1)} %copy-done, f32[1024]{0:T(1024)S(1)} %add_divide_fusion), kind=kOutput, calls=%fused_computation.54 | convolution fusion | flops 1610743808 | bytes 5246976 | tf_op jit(solution)/shard_map/dot_general | solution.py:57
  254.2 7.3 %fusion.38 = f32[1024,128]{1,0:T(8,128)S(1)} fusion(f32[1024,1024]{1,0:T(8,128)S(1)} %exponential_multiply_fusion.5, f32[1024,128]{1,0:T(8,128)S(1)} %copy-done, f32[1024]{0:T(1024)S(1)} %add_divide_fusion), kind=kOutput, calls=%fused_computation.56 | convolution fusion | flops 1610743808 | bytes 5246976 | tf_op jit(solution)/shard_map/dot_general | solution.py:57
  261.5 7.1 %fusion.40 = f32[1024,128]{1,0:T(8,128)S(1)} fusion(f32[1024,1024]{1,0:T(8,128)S(1)} %exponential_multiply_fusion.6, f32[1024,128]{1,0:T(8,128)S(1)} %copy-done, f32[1024]{0:T(1024)S(1)} %add_divide_fusion), kind=kOutput, calls=%fused_computation.58 | convolution fusion | flops 1610743808 | bytes 5246976 | tf_op jit(solution)/shard_map/dot_general | solution.py:57
  268.6 6.9 %fusion.34 = f32[1024,128]{1,0:T(8,128)S(1)} fusion(f32[1024,1024]{1,0:T(8,128)S(1)} %exponential_multiply_fusion.2, f32[1024,128]{1,0:T(8,128)S(1)} %copy-done, f32[1024]{0:T(1024)S(1)} %add_divide_fusion), kind=kOutput, calls=%fused_computation.52 | convolution fusion | flops 1610743808 | bytes 5246976 | tf_op jit(solution)/shard_map/dot_general | solution.py:57
  275.6 6.4 %collective-permute-start.24 = (f32[1024]{0:T(1024)S(1)}, f32[1024]{0:T(1024)S(1)}, u32[]{:S(2)}, u32[]{:S(2)}) collective-permute-start(f32[1024]{0:T(1024)S(1)} %bitcast.227), channel_id=1, source_target_pairs={{3,0},{4,1},{5,2},{6,3},{7,4},{8,5},{9,6},{10,7},{11,8},{12,9},{13... | collective-permute-start | bytes 12296 | tf_op jit(solution)/shard_map/ppermute | solution.py:21
  299.5 3.7 collective-permute-start.39
  303.1 5.9 %collective-permute-start.36 = (f32[1024,128]{1,0:T(8,128)S(1)}, f32[1024,128]{1,0:T(8,128)S(1)}, u32[]{:S(2)}, u32[]{:S(2)}) collective-permute-start(f32[1024,128]{1,0:T(8,128)S(1)} %fusion.40), channel_id=1, source_target_pairs={{3,0},{4,1},{5,2},{6,3},{7,4},{8,5},{9,6},{10,7},{11,8},{12,9},{13... | collective-permute-start | bytes 1572872 | tf_op jit(solution)/shard_map/ppermute | solution.py:21
  311.3 4.4 %collective-permute-start.38 = (f32[1024,128]{1,0:T(8,128)S(1)}, f32[1024,128]{1,0:T(8,128)S(1)}, u32[]{:S(2)}, u32[]{:S(2)}) collective-permute-start(f32[1024,128]{1,0:T(8,128)S(1)} %fusion.36), channel_id=1, source_target_pairs={{1,0},{2,1},{3,2},{4,3},{5,4},{6,5},{7,6},{8,7},{9,8},{10,9},{11,1... | collective-permute-start | bytes 1572872 | tf_op jit(solution)/shard_map/ppermute | solution.py:21
  325.3 6.5 %collective-permute-done.35 = f32[1024]{0:T(1024)S(1)} collective-permute-done((f32[1024]{0:T(1024)S(1)}, f32[1024]{0:T(1024)S(1)}, u32[]{:S(2)}, u32[]{:S(2)}) %collective-permute-start.35) | collective-permute-done | bytes 4128 | tf_op jit(solution)/shard_map/ppermute | solution.py:21
  341.1 10.1 %collective-permute-start.33 = (f32[1024]{0:T(1024)S(1)}, f32[1024]{0:T(1024)S(1)}, u32[]{:S(2)}, u32[]{:S(2)}) collective-permute-start(f32[1024]{0:T(1024)S(1)} %get-tuple-element.9), channel_id=1, source_target_pairs={{1,0},{2,1},{3,2},{4,3},{5,4},{6,5},{7,6},{8,7},{9,8},{10,9},{11,1... | collective-permute-start | bytes 12296 | tf_op jit(solution)/shard_map/ppermute | solution.py:21
  388.4 4.4 %collective-permute-done.30 = f32[1024]{0:T(1024)S(1)} collective-permute-done((f32[1024]{0:T(1024)S(1)}, f32[1024]{0:T(1024)S(1)}, u32[]{:S(2)}, u32[]{:S(2)}) %collective-permute-start.30) | collective-permute-done | bytes 4128 | tf_op jit(solution)/shard_map/ppermute | solution.py:21
  404.5 4.4 %fusion.10 = f32[1024,128]{1,0:T(8,128)} fusion(f32[1024,128]{1,0:T(8,128)S(1)} %fusion.11, f32[1024,128]{1,0:T(8,128)S(1)} %fusion.13, f32[1024,128]{1,0:T(8,128)S(1)} %fusion.1, f32[1024,1024]{1,0:T(8,128)S(1)} %exponential_multiply_fusion.2, f32[1024,128]{1,0:T(8,128)S(1)} %collective-permute-done.6, f32[1024]{0:T(1024)S(1)} %add_add_fusion, ...), kind=kOutput, calls=%fused_computation.20 | convolution fusion | flops 1611268096 | bytes 6823936 | tf_op jit(solution)/shard_map/dot_general | solution.py:50
  411.8 13.2 %collective-permute-done.41 = f32[1024,128]{1,0:T(8,128)S(1)} collective-permute-done((f32[1024,128]{1,0:T(8,128)S(1)}, f32[1024,128]{1,0:T(8,128)S(1)}, u32[]{:S(2)}, u32[]{:S(2)}) %collective-permute-start.41) | collective-permute-done | bytes 524320 | tf_op jit(solution)/shard_map/ppermute | solution.py:21
  424.9 7.8 %fusion.9 = f32[1024,128]{1,0:T(8,128)} fusion(f32[1024,128]{1,0:T(8,128)S(1)} %collective-permute-done.41, f32[1024,128]{1,0:T(8,128)S(1)} %collective-permute-done.40, f32[1024,128]{1,0:T(8,128)S(1)} %collective-permute-done.39, f32[1024,128]{1,0:T(8,128)S(1)} %collective-permute-done.38, f32[1024,128]{1,0:T(8,128)S(1)} %collective-permute-done.37, ...), kind=kOutput, calls=%fused_computation.19 | convolution fusion | flops 1611661312 | bytes 8396800 | tf_op jit(solution)/shard_map/dot_general | solution.py:57
  (139 shorter events, 221.3 us)
Async XLA Ops:
  1.3 47.8 %collective-permute-start.11 = (f32[1024]{0:T(1024)S(1)}, f32[1024]{0:T(1024)S(1)}, u32[]{:S(2)}, u32[]{:S(2)}) collective-permute-start(f32[1024]{0:T(1024)S(1)} %convert_element_type.19), channel_id=1, source_target_pairs={{3,0},{4,1},{5,2},{6,3},{7,4},{8,5},{9,6},{10,7},{11,8},{12,9},{13... | collective-permute-start | bytes 12296 | tf_op jit(solution)/shard_map/ppermute | solution.py:21
  9.9 116.9 %collective-permute-start.9 = (f32[1024]{0:T(1024)S(1)}, f32[1024]{0:T(1024)S(1)}, u32[]{:S(2)}, u32[]{:S(2)}) collective-permute-start(f32[1024]{0:T(1024)S(1)} %convert_element_type.19), channel_id=1, source_target_pairs={{2,0},{3,1},{4,2},{5,3},{6,4},{7,5},{8,6},{9,7},{10,8},{11,9},{12,... | collective-permute-start | bytes 12296 | tf_op jit(solution)/shard_map/ppermute | solution.py:21
  12.0 102.6 %collective-permute-start.7 = (f32[1024]{0:T(1024)S(1)}, f32[1024]{0:T(1024)S(1)}, u32[]{:S(2)}, u32[]{:S(2)}) collective-permute-start(f32[1024]{0:T(1024)S(1)} %convert_element_type.19), channel_id=1, source_target_pairs={{1,0},{2,1},{3,2},{4,3},{5,4},{6,5},{7,6},{8,7},{9,8},{10,9},{11,1... | collective-permute-start | bytes 12296 | tf_op jit(solution)/shard_map/ppermute | solution.py:21
  14.2 32.8 %collective-permute-start = (f32[1024,128]{1,0:T(8,128)}, f32[1024,128]{1,0:T(8,128)S(1)}, u32[]{:S(2)}, u32[]{:S(2)}) collective-permute-start(f32[1024,128]{1,0:T(8,128)} %param.9), channel_id=1, source_target_pairs={{0,3},{1,4},{2,5},{3,6},{4,7},{5,8},{6,9},{7,10},{8,11},{9,12},{10... | collective-permute-start | bytes 1572872 | tf_op jit(solution)/shard_map/ppermute | solution.py:21
  19.2 23.9 %collective-permute-start.10 = (f32[1024,128]{1,0:T(8,128)}, f32[1024,128]{1,0:T(8,128)S(1)}, u32[]{:S(2)}, u32[]{:S(2)}) collective-permute-start(f32[1024,128]{1,0:T(8,128)} %param.9), channel_id=1, source_target_pairs={{3,0},{4,1},{5,2},{6,3},{7,4},{8,5},{9,6},{10,7},{11,8},{12,9},{13... | collective-permute-start | bytes 1572872 | tf_op jit(solution)/shard_map/ppermute | solution.py:21
  43.1 67.0 %collective-permute-start.5 = (f32[1024]{0:T(1024)S(1)}, f32[1024]{0:T(1024)S(1)}, u32[]{:S(2)}, u32[]{:S(2)}) collective-permute-start(f32[1024]{0:T(1024)S(1)} %convert_element_type.19), channel_id=1, source_target_pairs={{0,1},{1,2},{2,3},{3,4},{4,5},{5,6},{6,7},{7,8},{8,9},{9,10},{10,1... | collective-permute-start | bytes 12296 | tf_op jit(solution)/shard_map/ppermute | solution.py:21
  47.0 50.3 %collective-permute-start.3 = (f32[1024]{0:T(1024)S(1)}, f32[1024]{0:T(1024)S(1)}, u32[]{:S(2)}, u32[]{:S(2)}) collective-permute-start(f32[1024]{0:T(1024)S(1)} %convert_element_type.19), channel_id=1, source_target_pairs={{0,2},{1,3},{2,4},{3,5},{4,6},{5,7},{6,8},{7,9},{8,10},{9,11},{10,... | collective-permute-start | bytes 12296 | tf_op jit(solution)/shard_map/ppermute | solution.py:21
  49.1 19.2 %collective-permute-start.2 = (f32[1024,128]{1,0:T(8,128)S(1)}, f32[1024,128]{1,0:T(8,128)S(1)}, u32[]{:S(2)}, u32[]{:S(2)}) collective-permute-start(f32[1024,128]{1,0:T(8,128)S(1)} %copy-done.1), channel_id=1, source_target_pairs={{0,2},{1,3},{2,4},{3,5},{4,6},{5,7},{6,8},{7,9},{8,10},{9,11},{10,... | collective-permute-start | bytes 1572872 | tf_op jit(solution)/shard_map/ppermute | solution.py:21
  88.0 38.6 %collective-permute-start.8 = (f32[1024,128]{1,0:T(8,128)S(1)}, f32[1024,128]{1,0:T(8,128)S(1)}, u32[]{:S(2)}, u32[]{:S(2)}) collective-permute-start(f32[1024,128]{1,0:T(8,128)S(1)} %copy-done.1), channel_id=1, source_target_pairs={{2,0},{3,1},{4,2},{5,3},{6,4},{7,5},{8,6},{9,7},{10,8},{11,9},{12,... | collective-permute-start | bytes 1572872 | tf_op jit(solution)/shard_map/ppermute | solution.py:21
  146.0 24.0 %collective-permute-start.12 = (f32[1024]{0:T(1024)S(1)}, f32[1024]{0:T(1024)S(1)}, u32[]{:S(2)}, u32[]{:S(2)}) collective-permute-start(f32[1024]{0:T(1024)S(1)} %bitcast.232), channel_id=1, source_target_pairs={{3,0},{4,1},{5,2},{6,3},{7,4},{8,5},{9,6},{10,7},{11,8},{12,9},{13... | collective-permute-start | bytes 12296 | tf_op jit(solution)/shard_map/ppermute | solution.py:21
  150.1 24.7 %collective-permute-start.13 = (f32[1024]{0:T(1024)S(1)}, f32[1024]{0:T(1024)S(1)}, u32[]{:S(2)}, u32[]{:S(2)}) collective-permute-start(f32[1024]{0:T(1024)S(1)} %bitcast.228), channel_id=1, source_target_pairs={{2,0},{3,1},{4,2},{5,3},{6,4},{7,5},{8,6},{9,7},{10,8},{11,9},{12,... | collective-permute-start | bytes 12296 | tf_op jit(solution)/shard_map/ppermute | solution.py:21
  179.1 17.5 %collective-permute-start.23 = (f32[1024]{0:T(1024)S(1)}, f32[1024]{0:T(1024)S(1)}, u32[]{:S(2)}, u32[]{:S(2)}) collective-permute-start(f32[1024]{0:T(1024)S(1)} %add_divide_fusion.1), channel_id=1, source_target_pairs={{3,0},{4,1},{5,2},{6,3},{7,4},{8,5},{9,6},{10,7},{11,8},{12,9},{13... | collective-permute-start | bytes 12296 | tf_op jit(solution)/shard_map/ppermute | solution.py:21
  182.1 21.8 %collective-permute-start.22 = (f32[1024]{0:T(1024)S(1)}, f32[1024]{0:T(1024)S(1)}, u32[]{:S(2)}, u32[]{:S(2)}) collective-permute-start(f32[1024]{0:T(1024)S(1)} %add_divide_fusion.1), channel_id=1, source_target_pairs={{2,0},{3,1},{4,2},{5,3},{6,4},{7,5},{8,6},{9,7},{10,8},{11,9},{12,... | collective-permute-start | bytes 12296 | tf_op jit(solution)/shard_map/ppermute | solution.py:21
  184.4 23.1 %collective-permute-start.21 = (f32[1024]{0:T(1024)S(1)}, f32[1024]{0:T(1024)S(1)}, u32[]{:S(2)}, u32[]{:S(2)}) collective-permute-start(f32[1024]{0:T(1024)S(1)} %add_divide_fusion.1), channel_id=1, source_target_pairs={{1,0},{2,1},{3,2},{4,3},{5,4},{6,5},{7,6},{8,7},{9,8},{10,9},{11,1... | collective-permute-start | bytes 12296 | tf_op jit(solution)/shard_map/ppermute | solution.py:21
  187.2 24.0 %collective-permute-start.20 = (f32[1024]{0:T(1024)S(1)}, f32[1024]{0:T(1024)S(1)}, u32[]{:S(2)}, u32[]{:S(2)}) collective-permute-start(f32[1024]{0:T(1024)S(1)} %add_divide_fusion.1), channel_id=1, source_target_pairs={{0,1},{1,2},{2,3},{3,4},{4,5},{5,6},{6,7},{7,8},{8,9},{9,10},{10,1... | collective-permute-start | bytes 12296 | tf_op jit(solution)/shard_map/ppermute | solution.py:21
  190.0 24.9 %collective-permute-start.19 = (f32[1024]{0:T(1024)S(1)}, f32[1024]{0:T(1024)S(1)}, u32[]{:S(2)}, u32[]{:S(2)}) collective-permute-start(f32[1024]{0:T(1024)S(1)} %add_divide_fusion.1), channel_id=1, source_target_pairs={{0,2},{1,3},{2,4},{3,5},{4,6},{5,7},{6,8},{7,9},{8,10},{9,11},{10,... | collective-permute-start | bytes 12296 | tf_op jit(solution)/shard_map/ppermute | solution.py:21
  196.6 22.3 %collective-permute-start.18 = (f32[1024]{0:T(1024)S(1)}, f32[1024]{0:T(1024)S(1)}, u32[]{:S(2)}, u32[]{:S(2)}) collective-permute-start(f32[1024]{0:T(1024)S(1)} %add_divide_fusion.1), channel_id=1, source_target_pairs={{0,3},{1,4},{2,5},{3,6},{4,7},{5,8},{6,9},{7,10},{8,11},{9,12},{10... | collective-permute-start | bytes 12296 | tf_op jit(solution)/shard_map/ppermute | solution.py:21
  275.6 19.3 %collective-permute-start.24 = (f32[1024]{0:T(1024)S(1)}, f32[1024]{0:T(1024)S(1)}, u32[]{:S(2)}, u32[]{:S(2)}) collective-permute-start(f32[1024]{0:T(1024)S(1)} %bitcast.227), channel_id=1, source_target_pairs={{3,0},{4,1},{5,2},{6,3},{7,4},{8,5},{9,6},{10,7},{11,8},{12,9},{13... | collective-permute-start | bytes 12296 | tf_op jit(solution)/shard_map/ppermute | solution.py:21
  284.0 15.4 %collective-permute-start.25 = (f32[1024]{0:T(1024)S(1)}, f32[1024]{0:T(1024)S(1)}, u32[]{:S(2)}, u32[]{:S(2)}) collective-permute-start(f32[1024]{0:T(1024)S(1)} %bitcast.231), channel_id=1, source_target_pairs={{2,0},{3,1},{4,2},{5,3},{6,4},{7,5},{8,6},{9,7},{10,8},{11,9},{12,... | collective-permute-start | bytes 12296 | tf_op jit(solution)/shard_map/ppermute | solution.py:21
  286.4 16.8 %collective-permute-start.26 = (f32[1024]{0:T(1024)S(1)}, f32[1024]{0:T(1024)S(1)}, u32[]{:S(2)}, u32[]{:S(2)}) collective-permute-start(f32[1024]{0:T(1024)S(1)} %bitcast.220), channel_id=1, source_target_pairs={{1,0},{2,1},{3,2},{4,3},{5,4},{6,5},{7,6},{8,7},{9,8},{10,9},{11,1... | collective-permute-start | bytes 12296 | tf_op jit(solution)/shard_map/ppermute | solution.py:21
  289.9 19.1 %collective-permute-start.27 = (f32[1024]{0:T(1024)S(1)}, f32[1024]{0:T(1024)S(1)}, u32[]{:S(2)}, u32[]{:S(2)}) collective-permute-start(f32[1024]{0:T(1024)S(1)} %bitcast.217), channel_id=1, source_target_pairs={{0,1},{1,2},{2,3},{3,4},{4,5},{5,6},{6,7},{7,8},{8,9},{9,10},{10,1... | collective-permute-start | bytes 12296 | tf_op jit(solution)/shard_map/ppermute | solution.py:21
  291.9 19.3 %collective-permute-start.28 = (f32[1024]{0:T(1024)S(1)}, f32[1024]{0:T(1024)S(1)}, u32[]{:S(2)}, u32[]{:S(2)}) collective-permute-start(f32[1024]{0:T(1024)S(1)} %bitcast.216), channel_id=1, source_target_pairs={{0,2},{1,3},{2,4},{3,5},{4,6},{5,7},{6,8},{7,9},{8,10},{9,11},{10,... | collective-permute-start | bytes 12296 | tf_op jit(solution)/shard_map/ppermute | solution.py:21
  294.9 20.8 %collective-permute-start.29 = (f32[1024]{0:T(1024)S(1)}, f32[1024]{0:T(1024)S(1)}, u32[]{:S(2)}, u32[]{:S(2)}) collective-permute-start(f32[1024]{0:T(1024)S(1)} %bitcast.215), channel_id=1, source_target_pairs={{0,3},{1,4},{2,5},{3,6},{4,7},{5,8},{6,9},{7,10},{8,11},{9,12},{10... | collective-permute-start | bytes 12296 | tf_op jit(solution)/shard_map/ppermute | solution.py:21
  299.5 102.8 %collective-permute-start.39 = (f32[1024,128]{1,0:T(8,128)S(1)}, f32[1024,128]{1,0:T(8,128)S(1)}, u32[]{:S(2)}, u32[]{:S(2)}) collective-permute-start(f32[1024,128]{1,0:T(8,128)S(1)} %fusion.34), channel_id=1, source_target_pairs={{0,1},{1,2},{2,3},{3,4},{4,5},{5,6},{6,7},{7,8},{8,9},{9,10},{10,1... | collective-permute-start | bytes 1572872 | tf_op jit(solution)/shard_map/ppermute | solution.py:21
  303.1 105.7 %collective-permute-start.36 = (f32[1024,128]{1,0:T(8,128)S(1)}, f32[1024,128]{1,0:T(8,128)S(1)}, u32[]{:S(2)}, u32[]{:S(2)}) collective-permute-start(f32[1024,128]{1,0:T(8,128)S(1)} %fusion.40), channel_id=1, source_target_pairs={{3,0},{4,1},{5,2},{6,3},{7,4},{8,5},{9,6},{10,7},{11,8},{12,9},{13... | collective-permute-start | bytes 1572872 | tf_op jit(solution)/shard_map/ppermute | solution.py:21
  309.0 99.8 %collective-permute-start.37 = (f32[1024,128]{1,0:T(8,128)S(1)}, f32[1024,128]{1,0:T(8,128)S(1)}, u32[]{:S(2)}, u32[]{:S(2)}) collective-permute-start(f32[1024,128]{1,0:T(8,128)S(1)} %fusion.38), channel_id=1, source_target_pairs={{2,0},{3,1},{4,2},{5,3},{6,4},{7,5},{8,6},{9,7},{10,8},{11,9},{12,... | collective-permute-start | bytes 1572872 | tf_op jit(solution)/shard_map/ppermute | solution.py:21
  311.3 97.6 %collective-permute-start.38 = (f32[1024,128]{1,0:T(8,128)S(1)}, f32[1024,128]{1,0:T(8,128)S(1)}, u32[]{:S(2)}, u32[]{:S(2)}) collective-permute-start(f32[1024,128]{1,0:T(8,128)S(1)} %fusion.36), channel_id=1, source_target_pairs={{1,0},{2,1},{3,2},{4,3},{5,4},{6,5},{7,6},{8,7},{9,8},{10,9},{11,1... | collective-permute-start | bytes 1572872 | tf_op jit(solution)/shard_map/ppermute | solution.py:21
  315.7 16.1 %collective-permute-start.35 = (f32[1024]{0:T(1024)S(1)}, f32[1024]{0:T(1024)S(1)}, u32[]{:S(2)}, u32[]{:S(2)}) collective-permute-start(f32[1024]{0:T(1024)S(1)} %get-tuple-element.9), channel_id=1, source_target_pairs={{3,0},{4,1},{5,2},{6,3},{7,4},{8,5},{9,6},{10,7},{11,8},{12,9},{13... | collective-permute-start | bytes 12296 | tf_op jit(solution)/shard_map/ppermute | solution.py:21
  341.1 17.3 %collective-permute-start.33 = (f32[1024]{0:T(1024)S(1)}, f32[1024]{0:T(1024)S(1)}, u32[]{:S(2)}, u32[]{:S(2)}) collective-permute-start(f32[1024]{0:T(1024)S(1)} %get-tuple-element.9), channel_id=1, source_target_pairs={{1,0},{2,1},{3,2},{4,3},{5,4},{6,5},{7,6},{8,7},{9,8},{10,9},{11,1... | collective-permute-start | bytes 12296 | tf_op jit(solution)/shard_map/ppermute | solution.py:21
  379.2 13.7 %collective-permute-start.30 = (f32[1024]{0:T(1024)S(1)}, f32[1024]{0:T(1024)S(1)}, u32[]{:S(2)}, u32[]{:S(2)}) collective-permute-start(f32[1024]{0:T(1024)S(1)} %get-tuple-element.9), channel_id=1, source_target_pairs={{0,3},{1,4},{2,5},{3,6},{4,7},{5,8},{6,9},{7,10},{8,11},{9,12},{10... | collective-permute-start | bytes 12296 | tf_op jit(solution)/shard_map/ppermute | solution.py:21
  392.9 18.9 %collective-permute-start.40 = (f32[1024,128]{1,0:T(8,128)S(1)}, f32[1024,128]{1,0:T(8,128)S(1)}, u32[]{:S(2)}, u32[]{:S(2)}) collective-permute-start(f32[1024,128]{1,0:T(8,128)S(1)} %fusion.32), channel_id=1, source_target_pairs={{0,2},{1,3},{2,4},{3,5},{4,6},{5,7},{6,8},{7,9},{8,10},{9,11},{10,... | collective-permute-start | bytes 1572872 | tf_op jit(solution)/shard_map/ppermute | solution.py:21
  402.3 22.7 %collective-permute-start.41 = (f32[1024,128]{1,0:T(8,128)S(1)}, f32[1024,128]{1,0:T(8,128)S(1)}, u32[]{:S(2)}, u32[]{:S(2)}) collective-permute-start(f32[1024,128]{1,0:T(8,128)S(1)} %fusion.30), channel_id=1, source_target_pairs={{0,3},{1,4},{2,5},{3,6},{4,7},{5,8},{6,9},{7,10},{8,11},{9,12},{10... | collective-permute-start | bytes 1572872 | tf_op jit(solution)/shard_map/ppermute | solution.py:21
  (14 other events, 162.7 us)
where the time goes:
time: 441 us; the launch traced here: 433 us
  matrix products  215 us (49%)
  starting transfers between devices  150 us (34%)
  waiting for transfers between devices  53.9 us (12%)
  between operations  6.96 us (2%)
  other arithmetic  6.72 us (2%)
    ppermute x42, starting transfers between devices, shifted(): return lax.ppermute(block, axis, route)  150 us
    ppermute x42, waiting for transfers between devices, shifted(): return lax.ppermute(block, axis, route)  53.9 us
    dot_general x14, matrix products, column_apply(): jnp.dot(kernel, scale_part, precision=highest, preferred_element_type=jnp...  51.3 us
    dot_general x7, matrix products, both_maps(): lax.dot_general(kernel, scaled_a, (((0,), (0,)), ((), ())), precision=hig...  50.2 us
    dot_general x7, matrix products, kernel_block(): lax.dot_general(left_unit, right_unit, (((1,), (1,)), ((), ())), precisio...  33.4 us
    dot_general x14, matrix products, row_apply(): jnp.dot(scale_part, kernel, precision=highest, preferred_element_type=jnp...  29.4 us
    dot_general x7, matrix products, both_maps(): jnp.dot(kernel, column_part, precision=highest, preferred_element_type=jn...  25.5 us
    dot_general x7, matrix products, both_maps(): jnp.dot(kernel, column_part[:, None] * raw_part, precision=highest, prefe...  25.5 us
  transfers between devices with their start and end apart: 42, of which 11 were waited for; matrix products, arithmetic and copies ran while one was open for 32% of the time, Pallas kernels for 0%

commit v1 on v0

v1 whole, which is shorter than its diff:
```python
import math
from functools import partial

import jax
import jax.numpy as jnp
import ml_dtypes
import numpy as np
from jax import lax
from jax.experimental import pallas as pl
from jax.experimental.pallas import tpu as pltpu
from jax.sharding import PartitionSpec as P

ROWS = 1024
WIDTH = 128
SLAB = 136
CATS = 16
OFFSETS = (0, 1, 2, -2, -3, -1, 3)
SLOT = {offset: slot for slot, offset in enumerate(OFFSETS)}
SLOTS = 7
SCALE = 10.0 * math.log2(math.e)
F32 = jnp.float32
BF16 = jnp.bfloat16
VMEM = pl.BlockSpec(memory_space=pltpu.VMEM)
SMEM = pl.BlockSpec(memory_space=pltpu.SMEM)
MIB = 1024 * 1024


def three_parts(value):
    parts = []
    for _ in range(3):
        part = float(np.float32(value).astype(ml_dtypes.bfloat16))
        parts.append(part)
        value = value - part
    return parts


MATCH = three_parts(0.5 * SCALE)
BASE = three_parts(-1.5 * SCALE)


def held(array):
    return pltpu.with_memory_space_constraint(array, pltpu.VMEM)


def inside(shape, dtype=F32):
    return pltpu.VMEM(shape, dtype)


def plain(shape, dtype=F32):
    return jax.ShapeDtypeStruct(shape, dtype)


def local(body, outs, operands, scratch=(), limit=8, scalars=0, name=None):
    return pl.pallas_call(
        body,
        out_shape=outs,
        in_specs=[SMEM] * scalars + [VMEM] * (len(operands) - scalars),
        out_specs=tuple(VMEM for _ in outs) if isinstance(outs, tuple) else VMEM,
        scratch_shapes=list(scratch),
        compiler_params=pltpu.CompilerParams(vmem_limit_bytes=limit * MIB),
        name=name,
    )(*operands)


def routed(block, target):
    devices = lax.axis_size("dev")
    route = [(i, target(i)) for i in range(devices) if 0 <= target(i) < devices]
    return lax.ppermute(block, "dev", route)


def partner(block):
    return routed(block, lambda i: i + 1 - 2 * (i % 2))


def beside(block):
    return routed(block, lambda i: i - 1 + 2 * (i % 2))


def toward(block, chips):
    return routed(block, lambda i: i - 2 * chips * (1 - 2 * (i % 2)))


def away(block, chips):
    return routed(block, lambda i: i + 2 * chips * (1 - 2 * (i % 2)))


def halves(x):
    high = x.astype(BF16)
    return high, (x - high.astype(F32)).astype(BF16)


def lanes_summed(x):
    total = x[:, 0:WIDTH]
    for j in range(1, x.shape[1] // WIDTH):
        total = total + x[:, j * WIDTH : (j + 1) * WIDTH]
    return total


def slab_body(b_ref, cat_ref, mass_ref, slab_ref):
    slab_ref[0:WIDTH, :] = b_ref[...].T
    pad = jnp.zeros((SLAB - WIDTH - 2, ROWS), F32)
    slab_ref[WIDTH:SLAB, :] = jnp.concatenate([cat_ref[...].astype(F32), mass_ref[...], pad], axis=0)


def left_body(a_ref, cat_ref, mass_ref, left_ref, wide_mass_ref):
    a = a_ref[...]
    unit = a * lax.rsqrt(jnp.sum(a * a, axis=1, keepdims=True) + 1e-06) * SCALE
    high, low = halves(unit)
    lane = lax.broadcasted_iota(jnp.int32, (ROWS, WIDTH), 1)
    cat = jnp.broadcast_to(cat_ref[...].astype(F32), (WIDTH, ROWS)).T
    same = (lane % CATS).astype(F32) == cat
    match = jnp.where(lane < CATS, MATCH[0], jnp.where(lane < 2 * CATS, MATCH[1], MATCH[2]))
    base = jnp.where(lane == 3 * CATS, BASE[0], jnp.where(lane == 3 * CATS + 1, BASE[1], BASE[2]))
    bias = jnp.where(
        lane < 3 * CATS, jnp.where(same, match, 0.0), jnp.where(lane < 3 * CATS + 3, base, 0.0)
    )
    left_ref[:, 0:128] = high
    left_ref[:, 128:256] = low
    left_ref[:, 256:384] = high
    left_ref[:, 384:512] = bias.astype(BF16)
    wide_mass_ref[...] = jnp.broadcast_to(mass_ref[...], (WIDTH, ROWS)).T


def block_body(slot, on_ref, left_ref, slab_ref, kernel_ref, sum_ref, mass_ref, right):
    mass_ref[...] = slab_ref[WIDTH:SLAB, :]
    on = on_ref[slot]

    @pl.when(on > 0)
    def _():
        v = slab_ref[0:WIDTH, :]
        v = v * lax.rsqrt(jnp.sum(v * v, axis=0, keepdims=True) + 1e-06)
        high, low = halves(v)
        row = lax.broadcasted_iota(jnp.int32, (WIDTH, ROWS), 0)
        same = (row % CATS).astype(F32) == slab_ref[WIDTH : WIDTH + 1, :]
        bias = jnp.where(row < 3 * CATS, same.astype(F32), (row < 3 * CATS + 3).astype(F32))
        right[0:128, :] = high
        right[128:256, :] = high
        right[256:384, :] = low
        right[384:512, :] = bias.astype(BF16)
        step = 256
        for i in range(ROWS // step):
            rows = slice(i * step, (i + 1) * step)
            kernel = jnp.exp2(jnp.dot(left_ref[rows, :], right[...], preferred_element_type=F32))
            kernel_ref[rows, :] = kernel
            sum_ref[rows, :] = lanes_summed(kernel)

    @pl.when(on == 0)
    def _():
        kernel_ref[...] = jnp.zeros((ROWS, ROWS), F32)
        sum_ref[...] = jnp.zeros((ROWS, WIDTH), F32)


def column_parts(kernels, scale_ref, part_ref):
    step = 32
    part_ref[7:8, :] = jnp.zeros((1, ROWS), F32)
    for slot, offset in enumerate(OFFSETS):

        def add(i, total, slot=slot):
            rows = pl.ds(pl.multiple_of(i * step, step), step)
            scale = scale_ref[rows, :]
            product = kernels[slot][rows, :] * jnp.concatenate([scale] * 8, axis=1)
            for t in range(step // 8):
                total = total + product[t * 8 : (t + 1) * 8]
            return total

        total = lax.fori_loop(0, ROWS // step, add, jnp.zeros((8, ROWS), F32), unroll=2)
        part_ref[3 + offset : 4 + offset, :] = jnp.sum(total, axis=0, keepdims=True)


def first_body(*refs):
    kernels, sums, (mass_ref, part_ref, scale) = refs[:7], refs[7:14], refs[14:]
    total = sums[0][...]
    for more in sums[1:]:
        total = total + more[...]
    scale[...] = mass_ref[...] / jnp.sum(total, axis=1, keepdims=True)
    column_parts(kernels, scale, part_ref)


def mirrored(x):
    return jnp.concatenate([x[7 - m : 8 - m] for m in range(8)], axis=0)


def chip_body(part_ref, other_ref, out_ref):
    out_ref[...] = part_ref[...] + mirrored(other_ref[...])


def upper_body(one_ref, two_ref, three_ref, out_ref):
    zeros = jnp.zeros((2, ROWS), F32)
    out = jnp.concatenate([zeros, one_ref[0:6, :]], axis=0)
    out = out + jnp.concatenate([zeros, zeros, two_ref[0:4, :]], axis=0)
    out_ref[...] = out + jnp.concatenate([zeros, zeros, zeros, three_ref[0:2, :]], axis=0)


def column_scales(totals, masses):
    chip_ref, near_ref, far_ref = totals
    total = chip_ref[...] + near_ref[...] + mirrored(far_ref[...])
    scales = []
    for slot, offset in enumerate(OFFSETS):
        here = total[3 + offset : 4 + offset]
        known = here > 0.0
        scales.append(jnp.where(known, masses[slot][1:2, :] / jnp.where(known, here, 1.0), 0.0))
    return scales


def second_body(*refs):
    kernels, totals, masses = refs[:7], refs[7:10], refs[10:17]
    mass_ref, scale_ref, part_ref, columns = refs[17:]
    for slot, scale in enumerate(column_scales(totals, masses)):
        columns[slot : slot + 1, :] = scale
    step = 32

    def add(i, carry):
        rows = pl.ds(pl.multiple_of(i * step, step), step)
        total = jnp.zeros((step, WIDTH), F32)
        for slot in range(SLOTS):
            total = total + lanes_summed(kernels[slot][rows, :] * columns[slot : slot + 1, :])
        scale_ref[rows, :] = mass_ref[rows, :] / jnp.sum(total, axis=1, keepdims=True)
        return carry

    lax.fori_loop(0, ROWS // step, add, 0)
    column_parts(kernels, scale_ref, part_ref)


def scaled_body(scale_ref, a_ref, out_ref):
    high, low = halves((scale_ref[...] * a_ref[...]).T)
    out_ref[0:128, :] = high
    out_ref[128:256, :] = low


def back_body(scaled_ref, kernel_ref, *rest):
    terms, out_ref = rest[:-1], rest[-1]
    step = 256
    for j in range(ROWS // step):
        columns = slice(j * step, (j + 1) * step)
        high, low = halves(kernel_ref[:, columns])
        wide = jnp.dot(scaled_ref[...], high, preferred_element_type=F32)
        out = jnp.dot(scaled_ref[0:128, :], low, preferred_element_type=F32)
        out = out + wide[0:128] + wide[128:256]
        for term in terms:
            out = out + term[:, columns]
        out_ref[:, columns] = out


def back_map(scaled, kernel, *terms):
    operands = (held(scaled), held(kernel), *terms)
    return local(back_body, plain((WIDTH, ROWS)), operands, name="back_map")


def ahead_body(*refs):
    kernels, slabs, totals, masses = refs[:7], refs[7:14], refs[14:17], refs[17:24]
    out_ref, sums, weights, right = refs[24:]
    step = 256
    for slot, scale in enumerate(column_scales(totals, masses)):
        high, low = halves(slabs[slot][0:WIDTH, :] * scale)
        right[0:128, :] = high
        right[128:256, :] = low
        for i in range(ROWS // step):
            rows = slice(i * step, (i + 1) * step)
            kernel = kernels[slot][rows, :]
            weight = lanes_summed(kernel * scale)
            high, low = halves(kernel)
            across = (((1,), (1,)), ((), ()))
            wide = lax.dot_general(high, right[...], across, preferred_element_type=F32)
            part = lax.dot_general(low, right[0:128, :], across, preferred_element_type=F32)
            part = part + wide[:, 0:128] + wide[:, 128:256]
            if slot > 0:
                part = part + sums[rows, :]
                weight = weight + weights[rows, :]
            if slot < SLOTS - 1:
                sums[rows, :] = part
                weights[rows, :] = weight
            else:
                out_ref[rows, :] = part / jnp.sum(weight, axis=1, keepdims=True)


def last_body(*refs):
    own_ref, one_ref, two_ref, chip_ref, near_ref, far_ref, out_ref = refs
    total = chip_ref[3:4, :] + near_ref[3:4, :] + far_ref[4:5, :]
    out_ref[...] = ((own_ref[...] + one_ref[...] + two_ref[...]) / total).T


def exchanged(part):
    chip = local(chip_body, plain((8, ROWS)), (part, partner(part)), limit=4, name="chip_sum")
    one, two, three = toward(chip, 1), toward(chip, 2), toward(chip, 3)
    near = local(upper_body, plain((8, ROWS)), (one, two, three), limit=4, name="near_sum")
    return chip, near, partner(near)


def shards(emb_a, emb_b, cat_a, cat_b, mass_a, mass_b, pair_list, pair_count):
    position = lax.axis_index("dev")
    usable = jnp.arange(SLOTS) < pair_count[0]
    sign = 1 - 2 * (position % 2)
    targets = position + sign * jnp.array(OFFSETS, jnp.int32)
    listed = (pair_list[0][None, :] == targets[:, None]) & usable[None, :]
    on = jnp.any(listed, axis=1).astype(jnp.int32)

    slab = local(
        slab_body, plain((SLAB, ROWS)), (emb_b, cat_b[None], mass_b[None]), name="slab"
    )
    ahead_one = toward(slab, 1)
    other = partner(slab)
    behind_one = away(slab, 1)
    third = beside(ahead_one)
    slabs = (slab, other, ahead_one, behind_one, third, partner(ahead_one), partner(behind_one))

    left, wide_mass = local(
        left_body,
        (inside((ROWS, 4 * WIDTH), BF16), inside((ROWS, WIDTH))),
        (emb_a, cat_a[None], mass_a[None]),
        name="left",
    )
    kernels, sums, masses = [], [], []
    for slot in range(SLOTS):
        kernel, row_sum, mass = local(
            partial(block_body, slot),
            (inside((ROWS, ROWS)), inside((ROWS, WIDTH)), plain((8, ROWS))),
            (on, held(left), slabs[slot]),
            [pltpu.VMEM((4 * WIDTH, ROWS), BF16)],
            scalars=1,
            name="kernel_block",
        )
        kernels.append(kernel)
        sums.append(row_sum)
        masses.append(mass)

    held_kernels = [held(kernel) for kernel in kernels]
    part = local(
        first_body,
        plain((8, ROWS)),
        (*held_kernels, *[held(x) for x in sums], held(wide_mass)),
        [pltpu.VMEM((ROWS, WIDTH), F32)],
        name="first_scales",
    )
    totals = exchanged(part)
    row_scale, part = local(
        second_body,
        (inside((ROWS, WIDTH)), plain((8, ROWS))),
        (*held_kernels, *totals, *masses, held(wide_mass)),
        [pltpu.VMEM((8, ROWS), F32)],
        name="second_scales",
    )
    totals = exchanged(part)
    scaled = local(
        scaled_body, inside((2 * WIDTH, ROWS), BF16), (held(row_scale), emb_a), name="scaled_a"
    )
    third = beside(back_map(scaled, kernels[SLOT[-3]]))
    behind = partner(back_map(scaled, kernels[SLOT[3]]))
    ahead = partner(back_map(scaled, kernels[SLOT[-1]]))
    home = partner(back_map(scaled, kernels[SLOT[1]]))
    one = toward(back_map(scaled, kernels[SLOT[-2]], behind), 1)
    two = away(back_map(scaled, kernels[SLOT[2]], ahead, third), 1)
    own = back_map(scaled, kernels[SLOT[0]], home)
    mapped_a = local(
        ahead_body,
        plain((ROWS, WIDTH)),
        (*held_kernels, *slabs, *totals, *masses),
        [pltpu.VMEM((ROWS, WIDTH), F32)] * 2 + [pltpu.VMEM((2 * WIDTH, ROWS), BF16)],
        limit=12,
        name="ahead_map",
    )
    mapped_b = local(last_body, plain((ROWS, WIDTH)), (own, one, two, *totals), name="last")
    return (mapped_a, mapped_b)


def solution(mesh):
    placed = (
        P("dev", None),
        P("dev", None),
        P("dev"),
        P("dev"),
        P("dev"),
        P("dev"),
        P("dev", None),
        P("dev"),
    )
    return jax.shard_map(
        shards,
        mesh=mesh,
        in_specs=placed,
        out_specs=(P("dev", None), P("dev", None)),
        check_vma=False,
    )
```

time: 441 us -> 143 us (0.32); the launches traced: 433 us -> 142 us
  matrix products: 215 us -> 0 us
  starting transfers between devices: 150 us -> 53.9 us
  Pallas kernels: 0 us -> 42.2 us
  waiting for transfers between devices: 53.9 us -> 33.2 us
  local copies, waits for them, and re-layouts: 0.02 us -> 9.22 us
  between operations: 6.96 us -> 1.71 us
  other arithmetic: 6.72 us -> 1.52 us
    dot_general x56 -> x0, matrix products: 215 us -> none  [the longest x14 51.3 us: column_apply(): jnp.dot(kernel, scale_part, precision=highest, preferred_element_type=jnp...]
    ppermute x42 -> x22, starting transfers between devices: 150 us -> 53.9 us  [routed(): return lax.ppermute(block, 'dev', route)]
    pallas_call x0 -> x25, Pallas kernels: none -> 42.2 us  [local(): pl.pallas_call(body, out_shape=outs, in_specs=[SMEM] * scalars + [VMEM] *...]
    ppermute x42 -> x22, waiting for transfers between devices: 53.9 us -> 33.2 us  [routed(): return lax.ppermute(block, 'dev', route)]
    unnamed x8 -> x28, local copies, waits for them, and re-layouts: 0.02 us -> 9.22 us
  transfers between devices with their start and end apart: 42 -> 22, of which waited for: 11 -> 13; matrix products, arithmetic and copies ran while one was open for 32% -> 1% of each run, Pallas kernels for 0% -> 18%
where the time goes in v1:
time: 143 us; the launch traced here: 142 us
  starting transfers between devices  53.9 us (38%)
  Pallas kernels  42.2 us (30%)
  waiting for transfers between devices  33.2 us (23%)
  local copies, waits for them, and re-layouts  9.22 us (6%)
  between operations  1.71 us (1%)
  other arithmetic  1.52 us (1%)
    ppermute x22, starting transfers between devices, routed(): return lax.ppermute(block, 'dev', route)  53.9 us
    pallas_call x25, Pallas kernels, local(): pl.pallas_call(body, out_shape=outs, in_specs=[SMEM] * scalars + [VMEM] *...  42.2 us
    ppermute x22, waiting for transfers between devices, routed(): return lax.ppermute(block, 'dev', route)  33.2 us
    unnamed x28, local copies, waits for them, and re-layouts  9.22 us
  transfers between devices with their start and end apart: 22, of which 13 were waited for; matrix products, arithmetic and copies ran while one was open for 1% of the time, Pallas kernels for 18%

profile of v1, /device:TPU:25, one launch (start us, length us, event | category | flops | bytes accessed | tf_op | source)
XLA Modules:
  0.0 141.7 jit_solution(2878714947581293555)
XLA Ops:
  3.3 8.0 %collective-permute-start.2 = (f32[136,1024]{1,0:T(8,128)S(1)}, f32[136,1024]{1,0:T(8,128)S(1)}, u32[]{:S(2)}, u32[]{:S(2)}) collective-permute-start(f32[136,1024]{1,0:T(8,128)S(1)} %slab.1.slab_ref.refs_7_), channel_id=1, source_target_pairs={{0,2},{2,4},{3,1},{4,6},{5,3},{6,8},{7,5},{8,10},{9,7},{10,12},{11... | collective-permute-start | bytes 1671176 | tf_op jit(solution)/shard_map/ppermute | solution.py:68
  11.3 1.9 %collective-permute-start.1 = (f32[136,1024]{1,0:T(8,128)S(1)}, f32[136,1024]{1,0:T(8,128)S(1)}, u32[]{:S(2)}, u32[]{:S(2)}) collective-permute-start(f32[136,1024]{1,0:T(8,128)S(1)} %slab.1.slab_ref.refs_7_), channel_id=1, source_target_pairs={{1,3},{2,0},{3,5},{4,2},{5,7},{6,4},{7,9},{8,6},{9,11},{10,8},{11,... | collective-permute-start | bytes 1671176 | tf_op jit(solution)/shard_map/ppermute | solution.py:68
  14.3 6.3 %collective-permute-done.2.slab_ref.refs_10_ = f32[136,1024]{1,0:T(8,128)S(1)} collective-permute-done((f32[136,1024]{1,0:T(8,128)S(1)}, f32[136,1024]{1,0:T(8,128)S(1)}, u32[]{:S(2)}, u32[]{:S(2)}) %collective-permute-start.2) | collective-permute-done | bytes 557088 | tf_op jit(solution)/shard_map/ppermute | solution.py:68
  20.6 5.2 %collective-permute-done.1.slab_ref.refs_9_ = f32[136,1024]{1,0:T(8,128)S(1)} collective-permute-done((f32[136,1024]{1,0:T(8,128)S(1)}, f32[136,1024]{1,0:T(8,128)S(1)}, u32[]{:S(2)}, u32[]{:S(2)}) %collective-permute-start.1) | collective-permute-done | bytes 557088 | tf_op jit(solution)/shard_map/ppermute | solution.py:68
  25.8 1.9 %collective-permute-start.3 = (f32[136,1024]{1,0:T(8,128)S(1)}, f32[136,1024]{1,0:T(8,128)}, u32[]{:S(2)}, u32[]{:S(2)}) collective-permute-start(f32[136,1024]{1,0:T(8,128)S(1)} %collective-permute-done.1.slab_ref.refs_9_), channel_id=1, source_target_pairs={{1,2},{2,1},{3,4},{4,3},{5,6},{6,5},{7,8},{8,7},{9,10},{10,9},{11,... | collective-permute-start | bytes 1671176 | tf_op jit(solution)/shard_map/ppermute | solution.py:68
  32.8 1.9 %kernel_block.7 = (f32[1024,1024]{1,0:T(8,128)S(1)}, f32[1024,128]{1,0:T(8,128)S(1)}, f32[8,1024]{1,0:T(8,128)S(1)}) custom-call(s32[7]{0:T(128)S(1)} %convert_element_type.3.on_ref, bf16[1024,512]{1,0:T(8,128)(2,1)S(1)} %get-tuple-element.27.left_ref, f32[136,1024]{1,0:T(8,128)S(1)} %slab.1.slab_ref.refs_7_), custom_call_target="tpu_custom_call" | custom-call | tf_op jit(solution)/shard_map/kernel_block/pallas_call | solution.py:54
  35.6 1.9 %kernel_block.9 = (f32[1024,1024]{1,0:T(8,128)S(1)}, f32[1024,128]{1,0:T(8,128)S(1)}, f32[8,1024]{1,0:T(8,128)S(1)}) custom-call(s32[7]{0:T(128)S(1)} %convert_element_type.3.on_ref, bf16[1024,512]{1,0:T(8,128)(2,1)S(1)} %get-tuple-element.27.left_ref, f32[136,1024]{1,0:T(8,128)S(1)} %collective-permute-done.1.slab_ref.refs_9_), custom_call_target="tpu_custom_call" | custom-call | tf_op jit(solution)/shard_map/kernel_block/pallas_call | solution.py:54
  38.4 1.9 %kernel_block.13 = (f32[1024,1024]{1,0:T(8,128)S(1)}, f32[1024,128]{1,0:T(8,128)S(1)}, f32[8,1024]{1,0:T(8,128)S(1)}) custom-call(s32[7]{0:T(128)S(1)} %convert_element_type.3.on_ref, bf16[1024,512]{1,0:T(8,128)(2,1)S(1)} %get-tuple-element.27.left_ref, f32[136,1024]{1,0:T(8,128)S(1)} %collective-permute-done.5.slab_ref.refs_13_), custom_call_target="tpu_custom_call" | custom-call | tf_op jit(solution)/shard_map/kernel_block/pallas_call | solution.py:54
  40.3 1.9 %kernel_block.12 = (f32[1024,1024]{1,0:T(8,128)S(1)}, f32[1024,128]{1,0:T(8,128)S(1)}, f32[8,1024]{1,0:T(8,128)S(1)}) custom-call(s32[7]{0:T(128)S(1)} %convert_element_type.3.on_ref, bf16[1024,512]{1,0:T(8,128)(2,1)S(1)} %get-tuple-element.27.left_ref, f32[136,1024]{1,0:T(8,128)S(1)} %collective-permute-done.4.slab_ref.refs_12_), custom_call_target="tpu_custom_call" | custom-call | tf_op jit(solution)/shard_map/kernel_block/pallas_call | solution.py:54
  42.2 2.6 %kernel_block.11 = (f32[1024,1024]{1,0:T(8,128)S(1)}, f32[1024,128]{1,0:T(8,128)S(1)}, f32[8,1024]{1,0:T(8,128)S(1)}) custom-call(s32[7]{0:T(128)S(1)} %convert_element_type.3.on_ref, bf16[1024,512]{1,0:T(8,128)(2,1)S(1)} %get-tuple-element.27.left_ref, f32[136,1024]{1,0:T(8,128)} %collective-permute-done.3.slab_ref.refs_11_), custom_call_target="tpu_custom_call" | custom-call | tf_op jit(solution)/shard_map/kernel_block/pallas_call | solution.py:54
  44.8 2.8 %first_scales.1.part_ref = f32[8,1024]{1,0:T(8,128)S(1)} custom-call(f32[1024,1024]{1,0:T(8,128)S(1)} %get-tuple-element.28.refs_0_.kernel_ref, f32[1024,1024]{1,0:T(8,128)S(1)} %get-tuple-element.29.refs_1_.kernel_ref, f32[1024,1024]{1,0:T(8,128)S(1)} %get-tuple-element.30.refs_2_.kernel_ref, f32[1024,1024]{1,0:T(8,128)S(1)} %get-tuple-element.31.refs_3_.kernel_ref, ...), custom_call_target="tpu_custom_call" | custom-call | tf_op jit(solution)/shard_map/first_scales/pallas_call | solution.py:54
  47.6 4.2 %collective-permute-start.6 = (f32[8,1024]{1,0:T(8,128)S(1)}, f32[8,1024]{1,0:T(8,128)S(1)}, u32[]{:S(2)}, u32[]{:S(2)}) collective-permute-start(f32[8,1024]{1,0:T(8,128)S(1)} %first_scales.1.part_ref), channel_id=1, source_target_pairs={{0,1},{1,0},{2,3},{3,2},{4,5},{5,4},{6,7},{7,6},{8,9},{9,8},{10,11... | collective-permute-start | bytes 98312 | tf_op jit(solution)/shard_map/ppermute | solution.py:68
  52.6 1.9 %collective-permute-start.9 = (f32[8,1024]{1,0:T(8,128)S(1)}, f32[8,1024]{1,0:T(8,128)S(1)}, u32[]{:S(2)}, u32[]{:S(2)}) collective-permute-start(f32[8,1024]{1,0:T(8,128)S(1)} %chip_sum.2.refs_7_), channel_id=1, source_target_pairs={{1,7},{3,9},{5,11},{6,0},{7,13},{8,2},{9,15},{10,4},{11,17},{12,6}... | collective-permute-start | bytes 98312 | tf_op jit(solution)/shard_map/ppermute | solution.py:68
  54.6 1.9 %collective-permute-start.8 = (f32[8,1024]{1,0:T(8,128)S(1)}, f32[8,1024]{1,0:T(8,128)S(1)}, u32[]{:S(2)}, u32[]{:S(2)}) collective-permute-start(f32[8,1024]{1,0:T(8,128)S(1)} %chip_sum.2.refs_7_), channel_id=1, source_target_pairs={{1,5},{3,7},{4,0},{5,9},{6,2},{7,11},{8,4},{9,13},{10,6},{11,15},{... | collective-permute-start | bytes 98312 | tf_op jit(solution)/shard_map/ppermute | solution.py:68
  56.5 1.9 %collective-permute-start.7 = (f32[8,1024]{1,0:T(8,128)S(1)}, f32[8,1024]{1,0:T(8,128)S(1)}, u32[]{:S(2)}, u32[]{:S(2)}) collective-permute-start(f32[8,1024]{1,0:T(8,128)S(1)} %chip_sum.2.refs_7_), channel_id=1, source_target_pairs={{1,3},{2,0},{3,5},{4,2},{5,7},{6,4},{7,9},{8,6},{9,11},{10,8},{11,... | collective-permute-start | bytes 98312 | tf_op jit(solution)/shard_map/ppermute | solution.py:68
  58.4 1.9 %collective-permute-done.9.three_ref = f32[8,1024]{1,0:T(8,128)S(1)} collective-permute-done((f32[8,1024]{1,0:T(8,128)S(1)}, f32[8,1024]{1,0:T(8,128)S(1)}, u32[]{:S(2)}, u32[]{:S(2)}) %collective-permute-start.9) | collective-permute-done | bytes 32800 | tf_op jit(solution)/shard_map/ppermute | solution.py:68
  60.3 3.4 %collective-permute-done.8.two_ref = f32[8,1024]{1,0:T(8,128)S(1)} collective-permute-done((f32[8,1024]{1,0:T(8,128)S(1)}, f32[8,1024]{1,0:T(8,128)S(1)}, u32[]{:S(2)}, u32[]{:S(2)}) %collective-permute-start.8) | collective-permute-done | bytes 32800 | tf_op jit(solution)/shard_map/ppermute | solution.py:68
  63.7 1.6 %collective-permute-done.7.one_ref = f32[8,1024]{1,0:T(8,128)S(1)} collective-permute-done((f32[8,1024]{1,0:T(8,128)S(1)}, f32[8,1024]{1,0:T(8,128)S(1)}, u32[]{:S(2)}, u32[]{:S(2)}) %collective-permute-start.7) | collective-permute-done | bytes 32800 | tf_op jit(solution)/shard_map/ppermute | solution.py:68
  66.9 2.2 %copy-done.3 = f32[1024,1024]{1,0:T(8,128)S(1)} copy-done((f32[1024,1024]{1,0:T(8,128)S(1)}, f32[1024,1024]{1,0:T(8,128)}, u32[]{:S(2)}) %copy-start.3) | copy-done | bytes 4194328
  69.1 2.2 %copy-done.6 = f32[1024,1024]{1,0:T(8,128)S(1)} copy-done((f32[1024,1024]{1,0:T(8,128)S(1)}, f32[1024,1024]{1,0:T(8,128)}, u32[]{:S(2)}) %copy-start.6) | copy-done | bytes 4194328
  71.3 7.7 %second_scales.1 = (f32[1024,128]{1,0:T(8,128)S(1)}, f32[8,1024]{1,0:T(8,128)S(1)}) custom-call(f32[1024,1024]{1,0:T(8,128)S(1)} %get-tuple-element.28.refs_0_.kernel_ref, f32[1024,1024]{1,0:T(8,128)S(1)} %get-tuple-element.29.refs_1_.kernel_ref, f32[1024,1024]{1,0:T(8,128)S(1)} %copy-done.6, f32[1024,1024]{1,0:T(8,128)S(1)} %copy-done.3, ...), custom_call_target="tpu_custom_call" | custom-call | tf_op jit(solution)/shard_map/second_scales/pallas_call | solution.py:54
  81.3 4.1 %collective-permute-start.20 = (f32[128,1024]{1,0:T(8,128)S(1)}, f32[128,1024]{1,0:T(8,128)S(1)}, u32[]{:S(2)}, u32[]{:S(2)}) collective-permute-start(f32[128,1024]{1,0:T(8,128)S(1)} %back_map.12), channel_id=1, source_target_pairs={{1,2},{2,1},{3,4},{4,3},{5,6},{6,5},{7,8},{8,7},{9,10},{10,9},{11,... | collective-permute-start | bytes 1572872 | tf_op jit(solution)/shard_map/ppermute | solution.py:68
  85.5 4.1 %collective-permute-start.19 = (f32[128,1024]{1,0:T(8,128)S(1)}, f32[128,1024]{1,0:T(8,128)S(1)}, u32[]{:S(2)}, u32[]{:S(2)}) collective-permute-start(f32[128,1024]{1,0:T(8,128)S(1)} %back_map.11), channel_id=1, source_target_pairs={{0,1},{1,0},{2,3},{3,2},{4,5},{5,4},{6,7},{7,6},{8,9},{9,8},{10,11... | collective-permute-start | bytes 1572872 | tf_op jit(solution)/shard_map/ppermute | solution.py:68
  93.7 11.5 %collective-permute-start.21 = (f32[128,1024]{1,0:T(8,128)S(1)}, f32[128,1024]{1,0:T(8,128)S(1)}, u32[]{:S(2)}, u32[]{:S(2)}) collective-permute-start(f32[128,1024]{1,0:T(8,128)S(1)} %back_map.13), channel_id=1, source_target_pairs={{0,2},{2,4},{3,1},{4,6},{5,3},{6,8},{7,5},{8,10},{9,7},{10,12},{11... | collective-permute-start | bytes 1572872 | tf_op jit(solution)/shard_map/ppermute | solution.py:68
  106.3 1.9 %collective-permute-start.18 = (f32[128,1024]{1,0:T(8,128)S(1)}, f32[128,1024]{1,0:T(8,128)S(1)}, u32[]{:S(2)}, u32[]{:S(2)}) collective-permute-start(f32[128,1024]{1,0:T(8,128)S(1)} %back_map.10), channel_id=1, source_target_pairs={{1,3},{2,0},{3,5},{4,2},{5,7},{6,4},{7,9},{8,6},{9,11},{10,8},{11,... | collective-permute-start | bytes 1572872 | tf_op jit(solution)/shard_map/ppermute | solution.py:68
  110.1 1.9 %collective-permute-start.14 = (f32[8,1024]{1,0:T(8,128)S(1)}, f32[8,1024]{1,0:T(8,128)S(1)}, u32[]{:S(2)}, u32[]{:S(2)}) collective-permute-start(f32[8,1024]{1,0:T(8,128)S(1)} %chip_sum.3.refs_14_.refs_3_), channel_id=1, source_target_pairs={{1,7},{3,9},{5,11},{6,0},{7,13},{8,2},{9,15},{10,4},{11,17},{12,6}... | collective-permute-start | bytes 98312 | tf_op jit(solution)/shard_map/ppermute | solution.py:68
  112.0 1.9 %collective-permute-start.13 = (f32[8,1024]{1,0:T(8,128)S(1)}, f32[8,1024]{1,0:T(8,128)S(1)}, u32[]{:S(2)}, u32[]{:S(2)}) collective-permute-start(f32[8,1024]{1,0:T(8,128)S(1)} %chip_sum.3.refs_14_.refs_3_), channel_id=1, source_target_pairs={{1,5},{3,7},{4,0},{5,9},{6,2},{7,11},{8,4},{9,13},{10,6},{11,15},{... | collective-permute-start | bytes 98312 | tf_op jit(solution)/shard_map/ppermute | solution.py:68
  114.0 3.8 %collective-permute-done.14.three_ref = f32[8,1024]{1,0:T(8,128)S(1)} collective-permute-done((f32[8,1024]{1,0:T(8,128)S(1)}, f32[8,1024]{1,0:T(8,128)S(1)}, u32[]{:S(2)}, u32[]{:S(2)}) %collective-permute-start.14) | collective-permute-done | bytes 32800 | tf_op jit(solution)/shard_map/ppermute | solution.py:68
  117.8 1.9 %collective-permute-start.12 = (f32[8,1024]{1,0:T(8,128)S(1)}, f32[8,1024]{1,0:T(8,128)S(1)}, u32[]{:S(2)}, u32[]{:S(2)}) collective-permute-start(f32[8,1024]{1,0:T(8,128)S(1)} %chip_sum.3.refs_14_.refs_3_), channel_id=1, source_target_pairs={{1,3},{2,0},{3,5},{4,2},{5,7},{6,4},{7,9},{8,6},{9,11},{10,8},{11,... | collective-permute-start | bytes 98312 | tf_op jit(solution)/shard_map/ppermute | solution.py:68
  119.7 1.5 %collective-permute-done.13.two_ref = f32[8,1024]{1,0:T(8,128)S(1)} collective-permute-done((f32[8,1024]{1,0:T(8,128)S(1)}, f32[8,1024]{1,0:T(8,128)S(1)}, u32[]{:S(2)}, u32[]{:S(2)}) %collective-permute-start.13) | collective-permute-done | bytes 32800 | tf_op jit(solution)/shard_map/ppermute | solution.py:68
  121.2 5.7 %collective-permute-done.12.one_ref = f32[8,1024]{1,0:T(8,128)S(1)} collective-permute-done((f32[8,1024]{1,0:T(8,128)S(1)}, f32[8,1024]{1,0:T(8,128)S(1)}, u32[]{:S(2)}, u32[]{:S(2)}) %collective-permute-start.12) | collective-permute-done | bytes 32800 | tf_op jit(solution)/shard_map/ppermute | solution.py:68
  129.1 10.6 %ahead_map.1 = f32[1024,128]{1,0:T(8,128)} custom-call(f32[1024,1024]{1,0:T(8,128)S(1)} %copy-done.1, f32[1024,1024]{1,0:T(8,128)S(1)} %get-tuple-element.29.refs_1_.kernel_ref, f32[1024,1024]{1,0:T(8,128)S(1)} %copy-done.7, f32[1024,1024]{1,0:T(8,128)S(1)} %copy-done.4, f32[1024,1024]{1,0:T(8,128)S(1)} %get-tuple-element.32.refs_4_.kernel_ref, ...), custom_call_target="tpu_custom_call" | custom-call | tf_op jit(solution)/shard_map/ahead_map/pallas_call | solution.py:54
  (69 shorter events, 25.8 us)
Async XLA Ops:
  0.6 1.0 copy-start.9
  3.3 17.3 %collective-permute-start.2 = (f32[136,1024]{1,0:T(8,128)S(1)}, f32[136,1024]{1,0:T(8,128)S(1)}, u32[]{:S(2)}, u32[]{:S(2)}) collective-permute-start(f32[136,1024]{1,0:T(8,128)S(1)} %slab.1.slab_ref.refs_7_), channel_id=1, source_target_pairs={{0,2},{2,4},{3,1},{4,6},{5,3},{6,8},{7,5},{8,10},{9,7},{10,12},{11... | collective-permute-start | bytes 1671176 | tf_op jit(solution)/shard_map/ppermute | solution.py:68
  11.3 14.5 %collective-permute-start.1 = (f32[136,1024]{1,0:T(8,128)S(1)}, f32[136,1024]{1,0:T(8,128)S(1)}, u32[]{:S(2)}, u32[]{:S(2)}) collective-permute-start(f32[136,1024]{1,0:T(8,128)S(1)} %slab.1.slab_ref.refs_7_), channel_id=1, source_target_pairs={{1,3},{2,0},{3,5},{4,2},{5,7},{6,4},{7,9},{8,6},{9,11},{10,8},{11,... | collective-permute-start | bytes 1671176 | tf_op jit(solution)/shard_map/ppermute | solution.py:68
  13.2 24.3 %collective-permute-start = (f32[136,1024]{1,0:T(8,128)S(1)}, f32[136,1024]{1,0:T(8,128)S(1)}, u32[]{:S(2)}, u32[]{:S(2)}) collective-permute-start(f32[136,1024]{1,0:T(8,128)S(1)} %slab.1.slab_ref.refs_7_), channel_id=1, source_target_pairs={{0,1},{1,0},{2,3},{3,2},{4,5},{5,4},{6,7},{7,6},{8,9},{9,8},{10,11... | collective-permute-start | bytes 1671176 | tf_op jit(solution)/shard_map/ppermute | solution.py:68
  20.6 17.8 %collective-permute-start.5 = (f32[136,1024]{1,0:T(8,128)S(1)}, f32[136,1024]{1,0:T(8,128)S(1)}, u32[]{:S(2)}, u32[]{:S(2)}) collective-permute-start(f32[136,1024]{1,0:T(8,128)S(1)} %collective-permute-done.2.slab_ref.refs_10_), channel_id=1, source_target_pairs={{0,1},{1,0},{2,3},{3,2},{4,5},{5,4},{6,7},{7,6},{8,9},{9,8},{10,11... | collective-permute-start | bytes 1671176 | tf_op jit(solution)/shard_map/ppermute | solution.py:68
  25.8 14.5 %collective-permute-start.4 = (f32[136,1024]{1,0:T(8,128)S(1)}, f32[136,1024]{1,0:T(8,128)S(1)}, u32[]{:S(2)}, u32[]{:S(2)}) collective-permute-start(f32[136,1024]{1,0:T(8,128)S(1)} %collective-permute-done.1.slab_ref.refs_9_), channel_id=1, source_target_pairs={{0,1},{1,0},{2,3},{3,2},{4,5},{5,4},{6,7},{7,6},{8,9},{9,8},{10,11... | collective-permute-start | bytes 1671176 | tf_op jit(solution)/shard_map/ppermute | solution.py:68
  25.8 16.4 %collective-permute-start.3 = (f32[136,1024]{1,0:T(8,128)S(1)}, f32[136,1024]{1,0:T(8,128)}, u32[]{:S(2)}, u32[]{:S(2)}) collective-permute-start(f32[136,1024]{1,0:T(8,128)S(1)} %collective-permute-done.1.slab_ref.refs_9_), channel_id=1, source_target_pairs={{1,2},{2,1},{3,4},{4,3},{5,6},{6,5},{7,8},{8,7},{9,10},{10,9},{11,... | collective-permute-start | bytes 1671176 | tf_op jit(solution)/shard_map/ppermute | solution.py:68
  29.9 1.0 copy-start.8
  34.7 32.2 %copy-start = (f32[1024,1024]{1,0:T(8,128)}, f32[1024,1024]{1,0:T(8,128)S(1)}, u32[]{:S(2)}) copy-start(f32[1024,1024]{1,0:T(8,128)S(1)} %get-tuple-element.28.refs_0_.kernel_ref) | copy-start | bytes 12582916
  35.6 12.0 %copy-start.2 = (f32[1024,1024]{1,0:T(8,128)}, f32[1024,1024]{1,0:T(8,128)S(1)}, u32[]{:S(2)}) copy-start(f32[1024,1024]{1,0:T(8,128)S(1)} %get-tuple-element.31.refs_3_.kernel_ref) | copy-start | bytes 12582916
  37.5 10.1 %copy-start.5 = (f32[1024,1024]{1,0:T(8,128)}, f32[1024,1024]{1,0:T(8,128)S(1)}, u32[]{:S(2)}) copy-start(f32[1024,1024]{1,0:T(8,128)S(1)} %get-tuple-element.30.refs_2_.kernel_ref) | copy-start | bytes 12582916
  47.6 5.0 %collective-permute-start.6 = (f32[8,1024]{1,0:T(8,128)S(1)}, f32[8,1024]{1,0:T(8,128)S(1)}, u32[]{:S(2)}, u32[]{:S(2)}) collective-permute-start(f32[8,1024]{1,0:T(8,128)S(1)} %first_scales.1.part_ref), channel_id=1, source_target_pairs={{0,1},{1,0},{2,3},{3,2},{4,5},{5,4},{6,7},{7,6},{8,9},{9,8},{10,11... | collective-permute-start | bytes 98312 | tf_op jit(solution)/shard_map/ppermute | solution.py:68
  52.6 7.7 %collective-permute-start.9 = (f32[8,1024]{1,0:T(8,128)S(1)}, f32[8,1024]{1,0:T(8,128)S(1)}, u32[]{:S(2)}, u32[]{:S(2)}) collective-permute-start(f32[8,1024]{1,0:T(8,128)S(1)} %chip_sum.2.refs_7_), channel_id=1, source_target_pairs={{1,7},{3,9},{5,11},{6,0},{7,13},{8,2},{9,15},{10,4},{11,17},{12,6}... | collective-permute-start | bytes 98312 | tf_op jit(solution)/shard_map/ppermute | solution.py:68
  54.6 9.2 %collective-permute-start.8 = (f32[8,1024]{1,0:T(8,128)S(1)}, f32[8,1024]{1,0:T(8,128)S(1)}, u32[]{:S(2)}, u32[]{:S(2)}) collective-permute-start(f32[8,1024]{1,0:T(8,128)S(1)} %chip_sum.2.refs_7_), channel_id=1, source_target_pairs={{1,5},{3,7},{4,0},{5,9},{6,2},{7,11},{8,4},{9,13},{10,6},{11,15},{... | collective-permute-start | bytes 98312 | tf_op jit(solution)/shard_map/ppermute | solution.py:68
  56.5 8.9 %collective-permute-start.7 = (f32[8,1024]{1,0:T(8,128)S(1)}, f32[8,1024]{1,0:T(8,128)S(1)}, u32[]{:S(2)}, u32[]{:S(2)}) collective-permute-start(f32[8,1024]{1,0:T(8,128)S(1)} %chip_sum.2.refs_7_), channel_id=1, source_target_pairs={{1,3},{2,0},{3,5},{4,2},{5,7},{6,4},{7,9},{8,6},{9,11},{10,8},{11,... | collective-permute-start | bytes 98312 | tf_op jit(solution)/shard_map/ppermute | solution.py:68
  65.4 1.5 %collective-permute-start.10 = (f32[8,1024]{1,0:T(8,128)S(1)}, f32[8,1024]{1,0:T(8,128)S(1)}, u32[]{:S(2)}, u32[]{:S(2)}) collective-permute-start(f32[8,1024]{1,0:T(8,128)S(1)} %near_sum.2.refs_8_), channel_id=1, source_target_pairs={{0,1},{1,0},{2,3},{3,2},{4,5},{5,4},{6,7},{7,6},{8,9},{9,8},{10,11... | collective-permute-start | bytes 98312 | tf_op jit(solution)/shard_map/ppermute | solution.py:68
  66.9 2.2 %copy-start.3 = (f32[1024,1024]{1,0:T(8,128)S(1)}, f32[1024,1024]{1,0:T(8,128)}, u32[]{:S(2)}) copy-start(f32[1024,1024]{1,0:T(8,128)} %copy-done.2) | copy-start | bytes 12582916
  69.1 2.2 %copy-start.6 = (f32[1024,1024]{1,0:T(8,128)S(1)}, f32[1024,1024]{1,0:T(8,128)}, u32[]{:S(2)}) copy-start(f32[1024,1024]{1,0:T(8,128)} %copy-done.5) | copy-start | bytes 12582916
  81.3 11.3 %copy-start.7 = (f32[1024,1024]{1,0:T(8,128)S(1)}, f32[1024,1024]{1,0:T(8,128)}, u32[]{:S(2)}) copy-start(f32[1024,1024]{1,0:T(8,128)} %copy-done.5) | copy-start | bytes 12582916
  81.3 11.3 %collective-permute-start.20 = (f32[128,1024]{1,0:T(8,128)S(1)}, f32[128,1024]{1,0:T(8,128)S(1)}, u32[]{:S(2)}, u32[]{:S(2)}) collective-permute-start(f32[128,1024]{1,0:T(8,128)S(1)} %back_map.12), channel_id=1, source_target_pairs={{1,2},{2,1},{3,4},{4,3},{5,6},{6,5},{7,8},{8,7},{9,10},{10,9},{11,... | collective-permute-start | bytes 1572872 | tf_op jit(solution)/shard_map/ppermute | solution.py:68
  85.5 7.1 %collective-permute-start.19 = (f32[128,1024]{1,0:T(8,128)S(1)}, f32[128,1024]{1,0:T(8,128)S(1)}, u32[]{:S(2)}, u32[]{:S(2)}) collective-permute-start(f32[128,1024]{1,0:T(8,128)S(1)} %back_map.11), channel_id=1, source_target_pairs={{0,1},{1,0},{2,3},{3,2},{4,5},{5,4},{6,7},{7,6},{8,9},{9,8},{10,11... | collective-permute-start | bytes 1572872 | tf_op jit(solution)/shard_map/ppermute | solution.py:68
  90.6 14.5 %collective-permute-start.17 = (f32[128,1024]{1,0:T(8,128)S(1)}, f32[128,1024]{1,0:T(8,128)S(1)}, u32[]{:S(2)}, u32[]{:S(2)}) collective-permute-start(f32[128,1024]{1,0:T(8,128)S(1)} %back_map.9), channel_id=1, source_target_pairs={{0,1},{1,0},{2,3},{3,2},{4,5},{5,4},{6,7},{7,6},{8,9},{9,8},{10,11... | collective-permute-start | bytes 1572872 | tf_op jit(solution)/shard_map/ppermute | solution.py:68
  91.8 13.4 %copy-start.4 = (f32[1024,1024]{1,0:T(8,128)S(1)}, f32[1024,1024]{1,0:T(8,128)}, u32[]{:S(2)}) copy-start(f32[1024,1024]{1,0:T(8,128)} %copy-done.2) | copy-start | bytes 12582916
  91.8 47.9 %collective-permute-start.16 = (f32[128,1024]{1,0:T(8,128)S(1)}, f32[128,1024]{1,0:T(8,128)S(1)}, u32[]{:S(2)}, u32[]{:S(2)}) collective-permute-start(f32[128,1024]{1,0:T(8,128)S(1)} %back_map.7), channel_id=1, source_target_pairs={{0,1},{1,0},{2,3},{3,2},{4,5},{5,4},{6,7},{7,6},{8,9},{9,8},{10,11... | collective-permute-start | bytes 1572872 | tf_op jit(solution)/shard_map/ppermute | solution.py:68
  93.7 35.4 %copy-start.1 = (f32[1024,1024]{1,0:T(8,128)S(1)}, f32[1024,1024]{1,0:T(8,128)}, u32[]{:S(2)}) copy-start(f32[1024,1024]{1,0:T(8,128)} %copy-done) | copy-start | bytes 12582916
  93.7 47.0 %collective-permute-start.21 = (f32[128,1024]{1,0:T(8,128)S(1)}, f32[128,1024]{1,0:T(8,128)S(1)}, u32[]{:S(2)}, u32[]{:S(2)}) collective-permute-start(f32[128,1024]{1,0:T(8,128)S(1)} %back_map.13), channel_id=1, source_target_pairs={{0,2},{2,4},{3,1},{4,6},{5,3},{6,8},{7,5},{8,10},{9,7},{10,12},{11... | collective-permute-start | bytes 1572872 | tf_op jit(solution)/shard_map/ppermute | solution.py:68
  106.3 34.5 %collective-permute-start.18 = (f32[128,1024]{1,0:T(8,128)S(1)}, f32[128,1024]{1,0:T(8,128)S(1)}, u32[]{:S(2)}, u32[]{:S(2)}) collective-permute-start(f32[128,1024]{1,0:T(8,128)S(1)} %back_map.10), channel_id=1, source_target_pairs={{1,3},{2,0},{3,5},{4,2},{5,7},{6,4},{7,9},{8,6},{9,11},{10,8},{11,... | collective-permute-start | bytes 1572872 | tf_op jit(solution)/shard_map/ppermute | solution.py:68
  108.2 1.9 %collective-permute-start.11 = (f32[8,1024]{1,0:T(8,128)S(1)}, f32[8,1024]{1,0:T(8,128)S(1)}, u32[]{:S(2)}, u32[]{:S(2)}) collective-permute-start(f32[8,1024]{1,0:T(8,128)S(1)} %get-tuple-element.50.part_ref), channel_id=1, source_target_pairs={{0,1},{1,0},{2,3},{3,2},{4,5},{5,4},{6,7},{7,6},{8,9},{9,8},{10,11... | collective-permute-start | bytes 98312 | tf_op jit(solution)/shard_map/ppermute | solution.py:68
  110.1 7.7 %collective-permute-start.14 = (f32[8,1024]{1,0:T(8,128)S(1)}, f32[8,1024]{1,0:T(8,128)S(1)}, u32[]{:S(2)}, u32[]{:S(2)}) collective-permute-start(f32[8,1024]{1,0:T(8,128)S(1)} %chip_sum.3.refs_14_.refs_3_), channel_id=1, source_target_pairs={{1,7},{3,9},{5,11},{6,0},{7,13},{8,2},{9,15},{10,4},{11,17},{12,6}... | collective-permute-start | bytes 98312 | tf_op jit(solution)/shard_map/ppermute | solution.py:68
  112.0 9.2 %collective-permute-start.13 = (f32[8,1024]{1,0:T(8,128)S(1)}, f32[8,1024]{1,0:T(8,128)S(1)}, u32[]{:S(2)}, u32[]{:S(2)}) collective-permute-start(f32[8,1024]{1,0:T(8,128)S(1)} %chip_sum.3.refs_14_.refs_3_), channel_id=1, source_target_pairs={{1,5},{3,7},{4,0},{5,9},{6,2},{7,11},{8,4},{9,13},{10,6},{11,15},{... | collective-permute-start | bytes 98312 | tf_op jit(solution)/shard_map/ppermute | solution.py:68
  117.8 9.2 %collective-permute-start.12 = (f32[8,1024]{1,0:T(8,128)S(1)}, f32[8,1024]{1,0:T(8,128)S(1)}, u32[]{:S(2)}, u32[]{:S(2)}) collective-permute-start(f32[8,1024]{1,0:T(8,128)S(1)} %chip_sum.3.refs_14_.refs_3_), channel_id=1, source_target_pairs={{1,3},{2,0},{3,5},{4,2},{5,7},{6,4},{7,9},{8,6},{9,11},{10,8},{11,... | collective-permute-start | bytes 98312 | tf_op jit(solution)/shard_map/ppermute | solution.py:68
  127.0 2.1 %collective-permute-start.15 = (f32[8,1024]{1,0:T(8,128)S(1)}, f32[8,1024]{1,0:T(8,128)S(1)}, u32[]{:S(2)}, u32[]{:S(2)}) collective-permute-start(f32[8,1024]{1,0:T(8,128)S(1)} %near_sum.3.refs_15_.refs_4_), channel_id=1, source_target_pairs={{0,1},{1,0},{2,3},{3,2},{4,5},{5,4},{6,7},{7,6},{8,9},{9,8},{10,11... | collective-permute-start | bytes 98312 | tf_op jit(solution)/shard_map/ppermute | solution.py:68
  (4 other events, 2.7 us)

commit v2 on v1

v2 whole, which is shorter than its diff:
```python
import math
from functools import partial

import jax
import jax.numpy as jnp
import ml_dtypes
import numpy as np
from jax import lax
from jax.experimental import pallas as pl
from jax.experimental.pallas import tpu as pltpu
from jax.sharding import PartitionSpec as P

ROWS = 1024
WIDTH = 128
SLAB = 136
CATS = 16
OFFSETS = (0, 1, 2, -2, -3, -1, 3)
SLOT = {offset: slot for slot, offset in enumerate(OFFSETS)}
SLOTS = 7
RELAYED = (2, 3)
SCALE = 10.0 * math.log2(math.e)
F32 = jnp.float32
BF16 = jnp.bfloat16
VMEM = pl.BlockSpec(memory_space=pltpu.VMEM)
SMEM = pl.BlockSpec(memory_space=pltpu.SMEM)
ANY = pl.BlockSpec(memory_space=pl.ANY)
MIB = 1024 * 1024


def three_parts(value):
    parts = []
    for _ in range(3):
        part = float(np.float32(value).astype(ml_dtypes.bfloat16))
        parts.append(part)
        value = value - part
    return parts


MATCH = three_parts(0.5 * SCALE)
BASE = three_parts(-1.5 * SCALE)


def held(array):
    return pltpu.with_memory_space_constraint(array, pltpu.VMEM)


def outside(array):
    return pltpu.with_memory_space_constraint(array, pltpu.HBM)


def inside(shape, dtype=F32):
    return pltpu.VMEM(shape, dtype)


def FLAGS(shape, dtype):
    return pltpu.SMEM(shape, dtype)


def flagged(array):
    return pltpu.with_memory_space_constraint(array, pltpu.SMEM)


def plain(shape, dtype=F32):
    return jax.ShapeDtypeStruct(shape, dtype)


def local(body, outs, operands, scratch=(), scalars=0, far=0, us=1, aliases=None, after=(), name=None):
    near = len(operands) - scalars - far
    used = len(operands)

    def with_tokens(*refs):
        body(*refs[:used], *refs[used + len(after) :])

    several = outs if isinstance(outs, tuple) else (outs,)
    spaces = [SMEM if getattr(out, "memory_space", None) is pltpu.SMEM else VMEM for out in several]
    return pl.pallas_call(
        with_tokens,
        out_shape=outs,
        in_specs=[SMEM] * scalars + [VMEM] * near + [ANY] * (far + len(after)),
        out_specs=tuple(spaces) if isinstance(outs, tuple) else spaces[0],
        scratch_shapes=list(scratch),
        input_output_aliases=aliases or {},
        compiler_params=pltpu.CompilerParams(vmem_limit_bytes=4 * MIB),
        cost_estimate=pl.CostEstimate(
            flops=int(us * 1e9), transcendentals=0, bytes_accessed=int(us * 3e6)
        ),
        name=name,
    )(*operands, *after)


def partner(block):
    devices = lax.axis_size("dev")
    return lax.ppermute(block, "dev", [(i, i + 1 - 2 * (i % 2)) for i in range(devices)])


def beside(block):
    devices = lax.axis_size("dev")
    route = [(i, (i - 1 + 2 * (i % 2)) % devices) for i in range(devices)]
    return lax.ppermute(block, "dev", route)


def relayed(block, chips, way):
    devices = lax.axis_size("dev")
    route = []
    for i in range(devices):
        target = i + 2 * chips * way * (1 - 2 * (i % 2))
        if target < 0:
            target = -1 - target
        if target >= devices:
            target = 2 * devices - 1 - target
        route.append((i, target))
    return lax.ppermute(block, "dev", route)


def toward(block, chips):
    return relayed(block, chips, -1)


def away(block, chips):
    return relayed(block, chips, 1)


def within(offset):
    position = lax.axis_index("dev")
    there = position + offset * (1 - 2 * (position % 2))
    return (there >= 0) & (there < lax.axis_size("dev"))


def halves(x):
    high = x.astype(BF16)
    return high, (x - high.astype(F32)).astype(BF16)


def lanes_summed(x):
    total = x[:, 0:WIDTH]
    for j in range(1, x.shape[1] // WIDTH):
        total = total + x[:, j * WIDTH : (j + 1) * WIDTH]
    return total


def fetch_all(copies, arrived):
    started = []
    for index, (source, target) in enumerate(copies):
        copy = pltpu.make_async_copy(source, target, arrived.at[index])
        copy.start()
        started.append(copy)
    for copy in started:
        copy.wait()


def slab_body(b_ref, cat_ref, mass_ref, slab_ref, b, cat, mass, arrived):
    fetch_all(((b_ref, b), (cat_ref, cat), (mass_ref, mass)), arrived)
    slab_ref[0:WIDTH, :] = b[...].T
    pad = jnp.zeros((SLAB - WIDTH - 2, ROWS), F32)
    slab_ref[WIDTH:SLAB, :] = jnp.concatenate([cat[...].astype(F32), mass[...], pad], axis=0)


def left_body(list_ref, count_ref, a_ref, cat_ref, mass_ref, *refs):
    left_ref, wide_mass_ref, on_ref, a, cat, mass, arrived = refs
    fetch_all(((a_ref, a), (cat_ref, cat), (mass_ref, mass)), arrived)
    position = lax.axis_index("dev")
    sign = 1 - 2 * (position % 2)
    for slot, offset in enumerate(OFFSETS):
        on = jnp.int32(0)
        for entry in range(SLOTS):
            here = (list_ref[0, entry] == position + sign * offset) & (entry < count_ref[0])
            on = jnp.where(here, jnp.int32(1), on)
        on_ref[slot] = on
    unit = a[...] * lax.rsqrt(jnp.sum(a[...] * a[...], axis=1, keepdims=True) + 1e-06) * SCALE
    high, low = halves(unit)
    lane = lax.broadcasted_iota(jnp.int32, (ROWS, WIDTH), 1)
    wide_cat = jnp.broadcast_to(cat[...].astype(F32), (WIDTH, ROWS)).T
    same = (lane % CATS).astype(F32) == wide_cat
    match = jnp.where(lane < CATS, MATCH[0], jnp.where(lane < 2 * CATS, MATCH[1], MATCH[2]))
    base = jnp.where(lane == 3 * CATS, BASE[0], jnp.where(lane == 3 * CATS + 1, BASE[1], BASE[2]))
    bias = jnp.where(
        lane < 3 * CATS, jnp.where(same, match, 0.0), jnp.where(lane < 3 * CATS + 3, base, 0.0)
    )
    left_ref[:, 0:128] = high
    left_ref[:, 128:256] = low
    left_ref[:, 256:384] = high
    left_ref[:, 384:512] = bias.astype(BF16)
    wide_mass_ref[...] = jnp.broadcast_to(mass[...], (WIDTH, ROWS)).T


def block_body(slot, on_ref, left_ref, slab_ref, *refs):
    kernel_ref, sum_ref, mass_ref = refs[-4 - (slot in RELAYED) :][:3]
    right = refs[-1]
    mass_ref[...] = slab_ref[WIDTH:SLAB, :]
    if slot in RELAYED:
        refs[-2][...] = slab_ref[...]

    @pl.when(on_ref[slot] > 0)
    def _():
        v = slab_ref[0:WIDTH, :]
        v = v * lax.rsqrt(jnp.sum(v * v, axis=0, keepdims=True) + 1e-06)
        high, low = halves(v)
        row = lax.broadcasted_iota(jnp.int32, (WIDTH, ROWS), 0)
        same = (row % CATS).astype(F32) == slab_ref[WIDTH : WIDTH + 1, :]
        bias = jnp.where(row < 3 * CATS, same.astype(F32), (row < 3 * CATS + 3).astype(F32))
        right[0:128, :] = high
        right[128:256, :] = high
        right[256:384, :] = low
        right[384:512, :] = bias.astype(BF16)
        step = 256
        for i in range(ROWS // step):
            rows = slice(i * step, (i + 1) * step)
            kernel = jnp.exp2(jnp.dot(left_ref[rows, :], right[...], preferred_element_type=F32))
            kernel_ref[slot, rows, :] = kernel
            total = lanes_summed(kernel)
            sum_ref[rows, :] = total if slot == 0 else sum_ref[rows, :] + total


def column_parts(on_ref, kernels, scale_ref, part_ref):
    step = 32
    part_ref[...] = jnp.zeros((8, ROWS), F32)
    for slot, offset in enumerate(OFFSETS):

        def add(i, total, slot=slot):
            rows = pl.ds(pl.multiple_of(i * step, step), step)
            scale = scale_ref[rows, :]
            product = kernels[slot, rows, :] * jnp.concatenate([scale] * 8, axis=1)
            for t in range(step // 8):
                total = total + product[t * 8 : (t + 1) * 8]
            return total

        @pl.when(on_ref[slot] > 0)
        def _(add=add, offset=offset):
            total = lax.fori_loop(0, ROWS // step, add, jnp.zeros((8, ROWS), F32), unroll=4)
            part_ref[3 + offset : 4 + offset, :] = jnp.sum(total, axis=0, keepdims=True)


def first_body(on_ref, kernels, sum_ref, mass_ref, kernels_out, part_ref, scale):
    scale[...] = mass_ref[...] / jnp.sum(sum_ref[...], axis=1, keepdims=True)
    column_parts(on_ref, kernels, scale, part_ref)


def mirrored(x):
    return jnp.concatenate([x[7 - m : 8 - m] for m in range(8)], axis=0)


def chip_body(part_ref, other_ref, out_ref):
    out_ref[...] = part_ref[...] + mirrored(other_ref[...])


def upper_body(one_ref, two_ref, three_ref, out_ref):
    out = jnp.zeros((8, ROWS), F32)
    for chips, ref in ((1, one_ref), (2, two_ref), (3, three_ref)):
        rows = jnp.where(within(2 * chips), ref[0 : 8 - 2 * chips, :], 0.0)
        out = out + jnp.concatenate([jnp.zeros((2 * chips, ROWS), F32), rows], axis=0)
    out_ref[...] = out


def column_scales(totals, masses):
    chip_ref, near_ref, far_ref = totals
    total = chip_ref[...] + near_ref[...] + mirrored(far_ref[...])
    scales = []
    for slot, offset in enumerate(OFFSETS):
        here = total[3 + offset : 4 + offset]
        known = here > 0.0
        scales.append(jnp.where(known, masses[slot][1:2, :] / jnp.where(known, here, 1.0), 0.0))
    return scales


def second_body(on_ref, kernels, *refs):
    totals, masses = refs[0:3], refs[3:10]
    mass_ref, kernels_out, scale_ref, part_ref = refs[10:]
    step = 32
    for slot, scale in enumerate(column_scales(totals, masses)):

        def add(i, carry, slot=slot, wide=jnp.broadcast_to(scale, (8, ROWS))):
            for t in range(0, step, 8):
                rows = pl.ds(pl.multiple_of(i * step + t, 8), 8)
                total = lanes_summed(kernels[slot, rows, :] * wide)
                scale_ref[rows, :] = total if slot == 0 else scale_ref[rows, :] + total
            return carry

        @pl.when(on_ref[slot] > 0)
        def _(add=add):
            lax.fori_loop(0, ROWS // step, add, 0, unroll=4)

    scale_ref[...] = mass_ref[...] / jnp.sum(scale_ref[...], axis=1, keepdims=True)
    column_parts(on_ref, kernels, scale_ref, part_ref)


def scaled_body(scale_ref, a_ref, out_ref):
    high, low = halves((scale_ref[...] * a_ref[...]).T)
    out_ref[0:128, :] = high
    out_ref[128:256, :] = low


def back_body(slot, on_ref, kernels, scaled_ref, *rest):
    terms, out_ref = rest[:-2], rest[-1]
    step = 256

    @pl.when(on_ref[slot] > 0)
    def _():
        for j in range(ROWS // step):
            columns = slice(j * step, (j + 1) * step)
            high, low = halves(kernels[slot, :, columns])
            wide = jnp.dot(scaled_ref[...], high, preferred_element_type=F32)
            out = jnp.dot(scaled_ref[0:128, :], low, preferred_element_type=F32)
            out = out + wide[0:128] + wide[128:256]
            for term in terms:
                out = out + term[:, columns]
            out_ref[:, columns] = out

    @pl.when(on_ref[slot] == 0)
    def _():
        out = jnp.zeros((WIDTH, ROWS), F32)
        for term in terms:
            out = out + term[...]
        out_ref[...] = out


def ahead_body(slot, last, on_ref, kernels, slab_ref, chip_ref, near_ref, far_ref, mass_ref, *refs):
    right = refs[-1]
    if last:
        sums, weights = refs[0:2]
        out_ref = refs[-2]
    else:
        sums, weights = refs[-3:-1]
    m = 3 + OFFSETS[slot]
    step = 256
    across = (((1,), (1,)), ((), ()))

    @pl.when(on_ref[slot] > 0)
    def _():
        total = chip_ref[m : m + 1, :] + near_ref[m : m + 1, :] + far_ref[7 - m : 8 - m, :]
        scale = mass_ref[1:2, :] / total
        high, low = halves(slab_ref[0:WIDTH, :] * scale)
        right[0:128, :] = high
        right[128:256, :] = low
        for i in range(ROWS // step):
            rows = slice(i * step, (i + 1) * step)
            kernel = kernels[slot, rows, :]
            weight = lanes_summed(kernel * scale)
            high, low = halves(kernel)
            wide = lax.dot_general(high, right[...], across, preferred_element_type=F32)
            part = lax.dot_general(low, right[0:128, :], across, preferred_element_type=F32)
            part = part + wide[:, 0:128] + wide[:, 128:256]
            sums[rows, :] = part if slot == 0 else part + sums[rows, :]
            weights[rows, :] = weight if slot == 0 else weight + weights[rows, :]

    if last:
        out_ref[...] = sums[...] / jnp.sum(weights[...], axis=1, keepdims=True)


def last_body(*refs):
    own_ref, one_ref, two_ref, chip_ref, near_ref, far_ref, out_ref = refs
    total = chip_ref[3:4, :] + near_ref[3:4, :] + far_ref[4:5, :]
    one = jnp.where(within(2), one_ref[...], 0.0)
    two = jnp.where(within(-2), two_ref[...], 0.0)
    out_ref[...] = ((own_ref[...] + one + two) / total).T


def exchanged(part):
    other = partner(part)
    chip = local(chip_body, plain((8, ROWS)), (part, other), name="chip_sum")
    one, two, three = toward(chip, 1), toward(chip, 2), toward(chip, 3)
    near = local(upper_body, plain((8, ROWS)), (one, two, three), name="near_sum")
    return (chip, near, partner(near)), (chip, three)


def shards(emb_a, emb_b, cat_a, cat_b, mass_a, mass_b, pair_list, pair_count):
    staged = [
        pltpu.VMEM((ROWS, WIDTH), F32),
        pltpu.VMEM((1, ROWS), jnp.int32),
        pltpu.VMEM((1, ROWS), F32),
        pltpu.SemaphoreType.DMA((3,)),
    ]
    slab = local(
        slab_body,
        plain((SLAB, ROWS)),
        tuple(map(outside, (emb_b, cat_b[None], mass_b[None]))),
        staged,
        far=3,
        name="slab",
    )
    ahead_one = toward(slab, 1)
    behind_one = away(slab, 1)
    other = partner(slab)
    left, wide_mass, on = local(
        left_body,
        (inside((ROWS, 4 * WIDTH), BF16), inside((ROWS, WIDTH)), FLAGS((8,), jnp.int32)),
        (pair_list, pair_count, *map(outside, (emb_a, cat_a[None], mass_a[None]))),
        staged,
        scalars=2,
        far=3,
        after=(slab,),
        name="left",
    )
    on = flagged(on)

    state, masses = (), [None] * SLOTS
    shapes = (inside((SLOTS, ROWS, ROWS)), inside((ROWS, WIDTH)), plain((8, ROWS)))

    def kernel_block(slot, slab):
        nonlocal state
        outs = shapes + ((plain((SLAB, ROWS)),) if slot in RELAYED else ())
        *state, masses[slot] = local(
            partial(block_body, slot),
            outs,
            (on, held(left), slab, *map(held, state)),
            [pltpu.VMEM((4 * WIDTH, ROWS), BF16)],
            scalars=1,
            us=2,
            aliases={3: 0, 4: 1} if state else None,
            name="kernel_block",
        )
        relayed = masses[slot]
        if slot in RELAYED:
            masses[slot] = state.pop()
        return relayed

    kernel_block(0, slab)
    kernel_block(1, other)
    shared_two = partner(kernel_block(3, behind_one))
    relayed = kernel_block(2, ahead_one)
    third = beside(relayed)
    shared = partner(relayed)
    kernel_block(6, shared_two)
    kernel_block(5, shared)
    kernel_block(4, third)
    slabs = (slab, other, ahead_one, behind_one, third, shared, shared_two)
    kernels, sums = state
    kernels, part = local(
        first_body,
        (shapes[0], plain((8, ROWS))),
        (on, held(kernels), held(sums), held(wide_mass)),
        [pltpu.VMEM((ROWS, WIDTH), F32)],
        scalars=1,
        us=3,
        aliases={1: 0},
        name="first_scales",
    )
    totals, _ = exchanged(part)
    kernels, row_scale, part = local(
        second_body,
        (shapes[0], inside((ROWS, WIDTH)), plain((8, ROWS))),
        (on, held(kernels), *totals, *masses, held(wide_mass)),
        scalars=1,
        us=5,
        aliases={1: 0},
        name="second_scales",
    )
    totals, steps = exchanged(part)
    scaled = local(
        scaled_body,
        inside((2 * WIDTH, ROWS), BF16),
        (held(row_scale), emb_a),
        after=steps[:1],
        name="scaled_a",
    )

    def back_map(offset, *terms, after=()):
        nonlocal kernels
        kernels, out = local(
            partial(back_body, SLOT[offset]),
            (shapes[0], plain((WIDTH, ROWS))),
            (on, held(kernels), held(scaled), *terms),
            scalars=1,
            us=2,
            aliases={1: 0},
            after=after,
            name="back_map",
        )
        return out

    third = beside(back_map(-3))
    behind = partner(back_map(3, after=totals[1:2]))
    ahead = partner(back_map(-1, after=totals[2:3]))
    home = partner(back_map(1))
    one = toward(back_map(-2, behind), 1)
    two = away(back_map(2, ahead, third), 1)
    state = ()
    for slot in range(SLOTS):
        last = slot == SLOTS - 1
        kernels, *state = local(
            partial(ahead_body, slot, last),
            (shapes[0], plain((ROWS, WIDTH))) if last else (shapes[0], shapes[1], shapes[1]),
            (on, held(kernels), slabs[slot], *totals, masses[slot], *map(held, state)),
            [pltpu.VMEM((2 * WIDTH, ROWS), BF16)],
            scalars=1,
            us=2,
            aliases={1: 0, 7: 1, 8: 2} if state and not last else {1: 0},
            name="ahead_map",
        )
    mapped_a = state[0]
    own = back_map(0, home)
    mapped_b = local(last_body, plain((ROWS, WIDTH)), (own, one, two, *totals), name="last")
    return (mapped_a, mapped_b)


def solution(mesh):
    placed = (
        P("dev", None),
        P("dev", None),
        P("dev"),
        P("dev"),
        P("dev"),
        P("dev"),
        P("dev", None),
        P("dev"),
    )
    return jax.shard_map(
        shards,
        mesh=mesh,
        in_specs=placed,
        out_specs=(P("dev", None), P("dev", None)),
        check_vma=False,
    )
```

time: 143 us -> 101 us (0.71)
  the two profiles are of different devices: /device:TPU:25 before, /device:TPU:16 now
where the time goes in v2:
time: 101 us; the launch traced here: 98.9 us
  starting transfers between devices  51.3 us (51%)
  waiting for transfers between devices  33.7 us (33%)
  Pallas kernels  11.7 us (12%)
  between operations  1.56 us (2%)
    ppermute x10, starting transfers between devices, relayed(): return lax.ppermute(block, 'dev', route)  26.6 us
    ppermute x10, waiting for transfers between devices, relayed(): return lax.ppermute(block, 'dev', route)  19.2 us
    ppermute x10, starting transfers between devices, partner(): lax.ppermute(block, 'dev', [(i, i + 1 - 2 * (i % 2)) for i in range(devic...  15.6 us
    pallas_call x31, Pallas kernels, local(): pl.pallas_call(with_tokens, out_shape=outs, in_specs=[SMEM] * scalars + [...  11.7 us
    ppermute x2, waiting for transfers between devices, beside(): return lax.ppermute(block, 'dev', route)  11.2 us
    ppermute x2, starting transfers between devices, beside(): return lax.ppermute(block, 'dev', route)  9.16 us
    ppermute x10, waiting for transfers between devices, partner(): lax.ppermute(block, 'dev', [(i, i + 1 - 2 * (i % 2)) for i in range(devic...  3.27 us
  transfers between devices with their start and end apart: 22, of which 10 were waited for; matrix products, arithmetic and copies ran while one was open for 0% of the time, Pallas kernels for 8%

profile of v2, /device:TPU:16, one launch (start us, length us, event | category | flops | bytes accessed | tf_op | source)
XLA Modules:
  0.0 98.9 jit_solution(6648600150621625640)
XLA Ops:
  0.6 1.3 %slab.1.refs_5_.refs_2_ = f32[136,1024]{1,0:T(8,128)S(1)} custom-call(f32[1024,128]{1,0:T(8,128)} %refs_0_.2, s32[1,1024]{1,0:T(1,128)} %bitcast.4, f32[1,1024]{1,0:T(1,128)} %bitcast.5), custom_call_target="tpu_custom_call" | custom-call | flops 1000000000 | bytes 3000000 | tf_op jit(solution)/shard_map/slab/pallas_call | solution.py:76
  2.0 2.0 %collective-permute-start.1 = (f32[136,1024]{1,0:T(8,128)S(1)}, f32[136,1024]{1,0:T(8,128)S(1)}, u32[]{:S(2)}, u32[]{:S(2)}) collective-permute-start(f32[136,1024]{1,0:T(8,128)S(1)} %slab.1.refs_5_.refs_2_), channel_id=1, source_target_pairs={{0,2},{1,0},{2,4},{3,1},{4,6},{5,3},{6,8},{7,5},{8,10},{9,7},{10,1... | collective-permute-start | bytes 1671176 | tf_op jit(solution)/shard_map/ppermute | solution.py:112
  4.0 4.3 %collective-permute-start = (f32[136,1024]{1,0:T(8,128)S(1)}, f32[136,1024]{1,0:T(8,128)S(1)}, u32[]{:S(2)}, u32[]{:S(2)}) collective-permute-start(f32[136,1024]{1,0:T(8,128)S(1)} %slab.1.refs_5_.refs_2_), channel_id=1, source_target_pairs={{0,1},{1,3},{2,0},{3,5},{4,2},{5,7},{6,4},{7,9},{8,6},{9,11},{10,8... | collective-permute-start | bytes 1671176 | tf_op jit(solution)/shard_map/ppermute | solution.py:112
  9.6 2.1 %left.1 = (bf16[1024,512]{1,0:T(8,128)(2,1)S(1)}, f32[1024,128]{1,0:T(8,128)S(1)}, s32[8]{0:T(128)S(4)}) custom-call(s32[1,7]{1,0:T(1,128)S(1)} %copy-done.1, s32[1]{0:T(128)S(6)} %copy.86.refs_1_, f32[1024,128]{1,0:T(8,128)} %refs_1_.2, s32[1,1024]{1,0:T(1,128)} %bitcast.6, f32[1,1024]{1,0:T(1,128)} %bitcast.7, f32[136,1024]{1,0:T(8,128)S(1)} %slab.1.refs_5_.refs_2_), custom_call_target="tpu_custom_call" | custom-call | flops 1000000000 | bytes 3000000 | tf_op jit(solution)/shard_map/left/pallas_call | solution.py:76
  11.8 1.3 %kernel_block.7 = (f32[7,1024,1024]{2,1,0:T(8,128)S(1)}, f32[1024,128]{1,0:T(8,128)S(1)}, f32[8,1024]{1,0:T(8,128)S(1)}) custom-call(s32[8]{0:T(128)S(4)} %get-tuple-element.66.refs_0_, bf16[1024,512]{1,0:T(8,128)(2,1)S(1)} %get-tuple-element.67.refs_1_, f32[136,1024]{1,0:T(8,128)S(1)} %slab.1.refs_5_.refs_2_), custom_call_target="tpu_custom_call" | custom-call | flops 2000000000 | bytes 6000000 | tf_op jit(solution)/shard_map/kernel_block/pallas_call | solution.py:76
  13.1 3.3 %collective-permute-done.1.refs_2_ = f32[136,1024]{1,0:T(8,128)S(1)} collective-permute-done((f32[136,1024]{1,0:T(8,128)S(1)}, f32[136,1024]{1,0:T(8,128)S(1)}, u32[]{:S(2)}, u32[]{:S(2)}) %collective-permute-start.1) | collective-permute-done | bytes 557088 | tf_op jit(solution)/shard_map/ppermute | solution.py:112
  16.5 5.2 %collective-permute-start.5 = (f32[136,1024]{1,0:T(8,128)S(1)}, f32[136,1024]{1,0:T(8,128)S(1)}, u32[]{:S(2)}, u32[]{:S(2)}) collective-permute-start(f32[136,1024]{1,0:T(8,128)S(1)} %get-tuple-element.75), channel_id=1, source_target_pairs={{0,1},{1,0},{2,3},{3,2},{4,5},{5,4},{6,7},{7,6},{8,9},{9,8},{10,11... | collective-permute-start | bytes 1671176 | tf_op jit(solution)/shard_map/ppermute | solution.py:93
  21.7 1.5 %collective-permute-start.4 = (f32[136,1024]{1,0:T(8,128)S(1)}, f32[136,1024]{1,0:T(8,128)S(1)}, u32[]{:S(2)}, u32[]{:S(2)}) collective-permute-start(f32[136,1024]{1,0:T(8,128)S(1)} %get-tuple-element.74), channel_id=1, source_target_pairs={{0,1},{1,0},{2,3},{3,2},{4,5},{5,4},{6,7},{7,6},{8,9},{9,8},{10,11... | collective-permute-start | bytes 1671176 | tf_op jit(solution)/shard_map/ppermute | solution.py:93
  23.1 6.8 %collective-permute-start.3 = (f32[136,1024]{1,0:T(8,128)S(1)}, f32[136,1024]{1,0:T(8,128)S(1)}, u32[]{:S(2)}, u32[]{:S(2)}) collective-permute-start(f32[136,1024]{1,0:T(8,128)S(1)} %get-tuple-element.74), channel_id=1, source_target_pairs={{0,127},{1,2},{2,1},{3,4},{4,3},{5,6},{6,5},{7,8},{8,7},{9,10},{10... | collective-permute-start | bytes 1671176 | tf_op jit(solution)/shard_map/ppermute | solution.py:99
  30.0 7.2 %collective-permute-done.3.refs_2_ = f32[136,1024]{1,0:T(8,128)S(1)} collective-permute-done((f32[136,1024]{1,0:T(8,128)S(1)}, f32[136,1024]{1,0:T(8,128)S(1)}, u32[]{:S(2)}, u32[]{:S(2)}) %collective-permute-start.3) | collective-permute-done | bytes 557088 | tf_op jit(solution)/shard_map/ppermute | solution.py:99
  37.8 1.2 %collective-permute-done.6.refs_1_ = f32[8,1024]{1,0:T(8,128)S(1)} collective-permute-done((f32[8,1024]{1,0:T(8,128)S(1)}, f32[8,1024]{1,0:T(8,128)S(1)}, u32[]{:S(2)}, u32[]{:S(2)}) %collective-permute-start.6) | collective-permute-done | bytes 32800 | tf_op jit(solution)/shard_map/ppermute | solution.py:93
  39.3 6.8 %collective-permute-start.8 = (f32[8,1024]{1,0:T(8,128)S(1)}, f32[8,1024]{1,0:T(8,128)S(1)}, u32[]{:S(2)}, u32[]{:S(2)}) collective-permute-start(f32[8,1024]{1,0:T(8,128)S(1)} %chip_sum.2.refs_2_), channel_id=1, source_target_pairs={{0,3},{1,5},{2,1},{3,7},{4,0},{5,9},{6,2},{7,11},{8,4},{9,13},{10,... | collective-permute-start | bytes 98312 | tf_op jit(solution)/shard_map/ppermute | solution.py:112
  46.1 2.3 %collective-permute-start.7 = (f32[8,1024]{1,0:T(8,128)S(1)}, f32[8,1024]{1,0:T(8,128)S(1)}, u32[]{:S(2)}, u32[]{:S(2)}) collective-permute-start(f32[8,1024]{1,0:T(8,128)S(1)} %chip_sum.2.refs_2_), channel_id=1, source_target_pairs={{0,1},{1,3},{2,0},{3,5},{4,2},{5,7},{6,4},{7,9},{8,6},{9,11},{10,8... | collective-permute-start | bytes 98312 | tf_op jit(solution)/shard_map/ppermute | solution.py:112
  48.4 3.2 %collective-permute-done.8.refs_1_ = f32[8,1024]{1,0:T(8,128)S(1)} collective-permute-done((f32[8,1024]{1,0:T(8,128)S(1)}, f32[8,1024]{1,0:T(8,128)S(1)}, u32[]{:S(2)}, u32[]{:S(2)}) %collective-permute-start.8) | collective-permute-done | bytes 32800 | tf_op jit(solution)/shard_map/ppermute | solution.py:112
  51.7 1.2 %collective-permute-done.10.refs_4_ = f32[8,1024]{1,0:T(8,128)S(1)} collective-permute-done((f32[8,1024]{1,0:T(8,128)S(1)}, f32[8,1024]{1,0:T(8,128)S(1)}, u32[]{:S(2)}, u32[]{:S(2)}) %collective-permute-start.10) | collective-permute-done | bytes 32800 | tf_op jit(solution)/shard_map/ppermute | solution.py:93
  52.9 1.0 %second_scales.1 = (f32[7,1024,1024]{2,1,0:T(8,128)S(1)}, f32[1024,128]{1,0:T(8,128)S(1)}, f32[8,1024]{1,0:T(8,128)S(1)}) custom-call(s32[8]{0:T(128)S(4)} %get-tuple-element.66.refs_0_, f32[7,1024,1024]{2,1,0:T(8,128)S(1)} %get-tuple-element.85.refs_1_, f32[8,1024]{1,0:T(8,128)S(1)} %chip_sum.2.refs_2_, ...), custom_call_target="tpu_custom_call", output_to_operand_aliasing={{0}: (1, {})} | custom-call | flops 5000000000 | bytes 15000000 | tf_op jit(solution)/shard_map/second_scales/pallas_call | solution.py:76
  53.9 2.8 %collective-permute-start.11 = (f32[8,1024]{1,0:T(8,128)S(1)}, f32[8,1024]{1,0:T(8,128)S(1)}, u32[]{:S(2)}, u32[]{:S(2)}) collective-permute-start(f32[8,1024]{1,0:T(8,128)S(1)} %get-tuple-element.96.refs_0_), channel_id=1, source_target_pairs={{0,1},{1,0},{2,3},{3,2},{4,5},{5,4},{6,7},{7,6},{8,9},{9,8},{10,11... | collective-permute-start | bytes 98312 | tf_op jit(solution)/shard_map/ppermute | solution.py:93
  57.7 1.6 %collective-permute-start.14 = (f32[8,1024]{1,0:T(8,128)S(1)}, f32[8,1024]{1,0:T(8,128)S(1)}, u32[]{:S(2)}, u32[]{:S(2)}) collective-permute-start(f32[8,1024]{1,0:T(8,128)S(1)} %chip_sum.3.refs_2_.refs_3_), channel_id=1, source_target_pairs={{0,5},{1,7},{2,3},{3,9},{4,1},{5,11},{6,0},{7,13},{8,2},{9,15},{10... | collective-permute-start | bytes 98312 | tf_op jit(solution)/shard_map/ppermute | solution.py:112
  59.3 3.5 %collective-permute-start.13 = (f32[8,1024]{1,0:T(8,128)S(1)}, f32[8,1024]{1,0:T(8,128)S(1)}, u32[]{:S(2)}, u32[]{:S(2)}) collective-permute-start(f32[8,1024]{1,0:T(8,128)S(1)} %chip_sum.3.refs_2_.refs_3_), channel_id=1, source_target_pairs={{0,3},{1,5},{2,1},{3,7},{4,0},{5,9},{6,2},{7,11},{8,4},{9,13},{10,... | collective-permute-start | bytes 98312 | tf_op jit(solution)/shard_map/ppermute | solution.py:112
  62.8 1.1 %collective-permute-start.12 = (f32[8,1024]{1,0:T(8,128)S(1)}, f32[8,1024]{1,0:T(8,128)S(1)}, u32[]{:S(2)}, u32[]{:S(2)}) collective-permute-start(f32[8,1024]{1,0:T(8,128)S(1)} %chip_sum.3.refs_2_.refs_3_), channel_id=1, source_target_pairs={{0,1},{1,3},{2,0},{3,5},{4,2},{5,7},{6,4},{7,9},{8,6},{9,11},{10,8... | collective-permute-start | bytes 98312 | tf_op jit(solution)/shard_map/ppermute | solution.py:112
  64.1 1.5 %collective-permute-done.14.refs_2_ = f32[8,1024]{1,0:T(8,128)S(1)} collective-permute-done((f32[8,1024]{1,0:T(8,128)S(1)}, f32[8,1024]{1,0:T(8,128)S(1)}, u32[]{:S(2)}, u32[]{:S(2)}) %collective-permute-start.14) | collective-permute-done | bytes 32800 | tf_op jit(solution)/shard_map/ppermute | solution.py:112
  65.6 1.6 %collective-permute-done.13.refs_1_ = f32[8,1024]{1,0:T(8,128)S(1)} collective-permute-done((f32[8,1024]{1,0:T(8,128)S(1)}, f32[8,1024]{1,0:T(8,128)S(1)}, u32[]{:S(2)}, u32[]{:S(2)}) %collective-permute-start.13) | collective-permute-done | bytes 32800 | tf_op jit(solution)/shard_map/ppermute | solution.py:112
  67.2 4.1 %collective-permute-start.15 = (f32[8,1024]{1,0:T(8,128)S(1)}, f32[8,1024]{1,0:T(8,128)S(1)}, u32[]{:S(2)}, u32[]{:S(2)}) collective-permute-start(f32[8,1024]{1,0:T(8,128)S(1)} %near_sum.3.refs_3_.refs_4_), channel_id=1, source_target_pairs={{0,1},{1,0},{2,3},{3,2},{4,5},{5,4},{6,7},{7,6},{8,9},{9,8},{10,11... | collective-permute-start | bytes 98312 | tf_op jit(solution)/shard_map/ppermute | solution.py:93
  71.4 2.4 %collective-permute-start.18 = (f32[128,1024]{1,0:T(8,128)S(1)}, f32[128,1024]{1,0:T(8,128)S(1)}, u32[]{:S(2)}, u32[]{:S(2)}) collective-permute-start(f32[128,1024]{1,0:T(8,128)S(1)} %get-tuple-element.104), channel_id=1, source_target_pairs={{0,127},{1,2},{2,1},{3,4},{4,3},{5,6},{6,5},{7,8},{8,7},{9,10},{10... | collective-permute-start | bytes 1572872 | tf_op jit(solution)/shard_map/ppermute | solution.py:99
  74.0 1.6 %collective-permute-start.19 = (f32[128,1024]{1,0:T(8,128)S(1)}, f32[128,1024]{1,0:T(8,128)S(1)}, u32[]{:S(2)}, u32[]{:S(2)}) collective-permute-start(f32[128,1024]{1,0:T(8,128)S(1)} %get-tuple-element.126), channel_id=1, source_target_pairs={{0,1},{1,0},{2,3},{3,2},{4,5},{5,4},{6,7},{7,6},{8,9},{9,8},{10,11... | collective-permute-start | bytes 1572872 | tf_op jit(solution)/shard_map/ppermute | solution.py:93
  75.6 4.7 %collective-permute-start.20 = (f32[128,1024]{1,0:T(8,128)S(1)}, f32[128,1024]{1,0:T(8,128)S(1)}, u32[]{:S(2)}, u32[]{:S(2)}) collective-permute-start(f32[128,1024]{1,0:T(8,128)S(1)} %get-tuple-element.128), channel_id=1, source_target_pairs={{0,1},{1,3},{2,0},{3,5},{4,2},{5,7},{6,4},{7,9},{8,6},{9,11},{10,8... | collective-permute-start | bytes 1572872 | tf_op jit(solution)/shard_map/ppermute | solution.py:112
  80.3 4.0 %collective-permute-done.18.refs_4_ = f32[128,1024]{1,0:T(8,128)S(1)} collective-permute-done((f32[128,1024]{1,0:T(8,128)S(1)}, f32[128,1024]{1,0:T(8,128)S(1)}, u32[]{:S(2)}, u32[]{:S(2)}) %collective-permute-start.18) | collective-permute-done | bytes 524320 | tf_op jit(solution)/shard_map/ppermute | solution.py:99
  84.4 1.6 %ahead_map.7 = (f32[7,1024,1024]{2,1,0:T(8,128)S(1)}, f32[1024,128]{1,0:T(8,128)S(1)}, f32[1024,128]{1,0:T(8,128)S(1)}) custom-call(s32[8]{0:T(128)S(4)} %get-tuple-element.66.refs_0_, f32[7,1024,1024]{2,1,0:T(8,128)S(1)} %get-tuple-element.105.refs_1_, f32[136,1024]{1,0:T(8,128)S(1)} %slab.1.refs_5_.refs_2_, ...), custom_call_target="tpu_custom_call", output_to_operand_aliasing={{0}: (1, {})} | custom-call | flops 2000000000 | bytes 6000000 | tf_op jit(solution)/shard_map/ahead_map/pallas_call | solution.py:76
  86.1 1.0 %ahead_map.13 = (f32[7,1024,1024]{2,1,0:T(8,128)S(1)}, f32[1024,128]{1,0:T(8,128)}) custom-call(s32[8]{0:T(128)S(4)} %get-tuple-element.66.refs_0_, f32[7,1024,1024]{2,1,0:T(8,128)S(1)} %get-tuple-element.121.refs_1_, f32[136,1024]{1,0:T(8,128)S(1)} %collective-permute-done.5.refs_2_, ...), custom_call_target="tpu_custom_call", output_to_operand_aliasing={{0}: (1, {})} | custom-call | flops 2000000000 | bytes 6000000 | tf_op jit(solution)/shard_map/ahead_map/pallas_call | solution.py:76
  87.1 1.1 %back_map.13 = (f32[7,1024,1024]{2,1,0:T(8,128)S(1)}, f32[128,1024]{1,0:T(8,128)S(1)}) custom-call(s32[8]{0:T(128)S(4)} %get-tuple-element.66.refs_0_, f32[7,1024,1024]{2,1,0:T(8,128)S(1)} %get-tuple-element.125.refs_1_, bf16[256,1024]{1,0:T(8,128)(2,1)S(1)} %scaled_a.1.refs_2_, ...), custom_call_target="tpu_custom_call", output_to_operand_aliasing={{0}: (1, {})} | custom-call | flops 2000000000 | bytes 6000000 | tf_op jit(solution)/shard_map/back_map/pallas_call | solution.py:76
  88.2 9.6 %collective-permute-done.21.refs_2_ = f32[128,1024]{1,0:T(8,128)S(1)} collective-permute-done((f32[128,1024]{1,0:T(8,128)S(1)}, f32[128,1024]{1,0:T(8,128)S(1)}, u32[]{:S(2)}, u32[]{:S(2)}) %collective-permute-start.21) | collective-permute-done | bytes 524320 | tf_op jit(solution)/shard_map/ppermute | solution.py:112
  97.8 1.0 %last.1 = f32[1024,128]{1,0:T(8,128)} custom-call(f32[128,1024]{1,0:T(8,128)S(1)} %get-tuple-element.127.refs_0_, f32[128,1024]{1,0:T(8,128)S(1)} %collective-permute-done.20.refs_1_, f32[128,1024]{1,0:T(8,128)S(1)} %collective-permute-done.21.refs_2_, f32[8,1024]{1,0:T(8,128)S(1)} %chip_sum.3.refs_2_.refs_3_, f32[8,1024]{1,0:T(8,128)S(1)} %near_sum.3.refs_3_.refs_4_, ...), custom_call_target="tpu_custom_call" | custom-call | flops 1000000000 | bytes 3000000 | tf_op jit(solution)/shard_map/last/pallas_call | solution.py:76
  (47 shorter events, 3.6 us)
Async XLA Ops:
  1.9 11.2 %collective-permute-start.2 = (f32[136,1024]{1,0:T(8,128)S(1)}, f32[136,1024]{1,0:T(8,128)S(1)}, u32[]{:S(2)}, u32[]{:S(2)}) collective-permute-start(f32[136,1024]{1,0:T(8,128)S(1)} %slab.1.refs_5_.refs_2_), channel_id=1, source_target_pairs={{0,1},{1,0},{2,3},{3,2},{4,5},{5,4},{6,7},{7,6},{8,9},{9,8},{10,11... | collective-permute-start | bytes 1671176 | tf_op jit(solution)/shard_map/ppermute | solution.py:93
  2.0 14.4 %collective-permute-start.1 = (f32[136,1024]{1,0:T(8,128)S(1)}, f32[136,1024]{1,0:T(8,128)S(1)}, u32[]{:S(2)}, u32[]{:S(2)}) collective-permute-start(f32[136,1024]{1,0:T(8,128)S(1)} %slab.1.refs_5_.refs_2_), channel_id=1, source_target_pairs={{0,2},{1,0},{2,4},{3,1},{4,6},{5,3},{6,8},{7,5},{8,10},{9,7},{10,1... | collective-permute-start | bytes 1671176 | tf_op jit(solution)/shard_map/ppermute | solution.py:112
  4.0 17.6 %collective-permute-start = (f32[136,1024]{1,0:T(8,128)S(1)}, f32[136,1024]{1,0:T(8,128)S(1)}, u32[]{:S(2)}, u32[]{:S(2)}) collective-permute-start(f32[136,1024]{1,0:T(8,128)S(1)} %slab.1.refs_5_.refs_2_), channel_id=1, source_target_pairs={{0,1},{1,3},{2,0},{3,5},{4,2},{5,7},{6,4},{7,9},{8,6},{9,11},{10,8... | collective-permute-start | bytes 1671176 | tf_op jit(solution)/shard_map/ppermute | solution.py:112
  9.0 0.7 copy-start.1
  16.5 13.5 %collective-permute-start.5 = (f32[136,1024]{1,0:T(8,128)S(1)}, f32[136,1024]{1,0:T(8,128)S(1)}, u32[]{:S(2)}, u32[]{:S(2)}) collective-permute-start(f32[136,1024]{1,0:T(8,128)S(1)} %get-tuple-element.75), channel_id=1, source_target_pairs={{0,1},{1,0},{2,3},{3,2},{4,5},{5,4},{6,7},{7,6},{8,9},{9,8},{10,11... | collective-permute-start | bytes 1671176 | tf_op jit(solution)/shard_map/ppermute | solution.py:93
  21.7 8.3 %collective-permute-start.4 = (f32[136,1024]{1,0:T(8,128)S(1)}, f32[136,1024]{1,0:T(8,128)S(1)}, u32[]{:S(2)}, u32[]{:S(2)}) collective-permute-start(f32[136,1024]{1,0:T(8,128)S(1)} %get-tuple-element.74), channel_id=1, source_target_pairs={{0,1},{1,0},{2,3},{3,2},{4,5},{5,4},{6,7},{7,6},{8,9},{9,8},{10,11... | collective-permute-start | bytes 1671176 | tf_op jit(solution)/shard_map/ppermute | solution.py:93
  23.1 14.0 %collective-permute-start.3 = (f32[136,1024]{1,0:T(8,128)S(1)}, f32[136,1024]{1,0:T(8,128)S(1)}, u32[]{:S(2)}, u32[]{:S(2)}) collective-permute-start(f32[136,1024]{1,0:T(8,128)S(1)} %get-tuple-element.74), channel_id=1, source_target_pairs={{0,127},{1,2},{2,1},{3,4},{4,3},{5,6},{6,5},{7,8},{8,7},{9,10},{10... | collective-permute-start | bytes 1671176 | tf_op jit(solution)/shard_map/ppermute | solution.py:99
  37.1 26.7 %copy-start = (f32[1024,128]{1,0:T(8,128)S(1)}, f32[1024,128]{1,0:T(8,128)}, u32[]{:S(2)}) copy-start(f32[1024,128]{1,0:T(8,128)} %refs_1_.2) | copy-start | bytes 1572868
  37.7 1.3 %collective-permute-start.6 = (f32[8,1024]{1,0:T(8,128)S(1)}, f32[8,1024]{1,0:T(8,128)S(1)}, u32[]{:S(2)}, u32[]{:S(2)}) collective-permute-start(f32[8,1024]{1,0:T(8,128)S(1)} %get-tuple-element.86.refs_0_), channel_id=1, source_target_pairs={{0,1},{1,0},{2,3},{3,2},{4,5},{5,4},{6,7},{7,6},{8,9},{9,8},{10,11... | collective-permute-start | bytes 98312 | tf_op jit(solution)/shard_map/ppermute | solution.py:93
  39.1 9.3 %collective-permute-start.9 = (f32[8,1024]{1,0:T(8,128)S(1)}, f32[8,1024]{1,0:T(8,128)S(1)}, u32[]{:S(2)}, u32[]{:S(2)}) collective-permute-start(f32[8,1024]{1,0:T(8,128)S(1)} %chip_sum.2.refs_2_), channel_id=1, source_target_pairs={{0,5},{1,7},{2,3},{3,9},{4,1},{5,11},{6,0},{7,13},{8,2},{9,15},{10... | collective-permute-start | bytes 98312 | tf_op jit(solution)/shard_map/ppermute | solution.py:112
  39.3 12.3 %collective-permute-start.8 = (f32[8,1024]{1,0:T(8,128)S(1)}, f32[8,1024]{1,0:T(8,128)S(1)}, u32[]{:S(2)}, u32[]{:S(2)}) collective-permute-start(f32[8,1024]{1,0:T(8,128)S(1)} %chip_sum.2.refs_2_), channel_id=1, source_target_pairs={{0,3},{1,5},{2,1},{3,7},{4,0},{5,9},{6,2},{7,11},{8,4},{9,13},{10,... | collective-permute-start | bytes 98312 | tf_op jit(solution)/shard_map/ppermute | solution.py:112
  46.1 5.5 %collective-permute-start.7 = (f32[8,1024]{1,0:T(8,128)S(1)}, f32[8,1024]{1,0:T(8,128)S(1)}, u32[]{:S(2)}, u32[]{:S(2)}) collective-permute-start(f32[8,1024]{1,0:T(8,128)S(1)} %chip_sum.2.refs_2_), channel_id=1, source_target_pairs={{0,1},{1,3},{2,0},{3,5},{4,2},{5,7},{6,4},{7,9},{8,6},{9,11},{10,8... | collective-permute-start | bytes 98312 | tf_op jit(solution)/shard_map/ppermute | solution.py:112
  51.6 1.3 %collective-permute-start.10 = (f32[8,1024]{1,0:T(8,128)S(1)}, f32[8,1024]{1,0:T(8,128)S(1)}, u32[]{:S(2)}, u32[]{:S(2)}) collective-permute-start(f32[8,1024]{1,0:T(8,128)S(1)} %near_sum.2.refs_3_), channel_id=1, source_target_pairs={{0,1},{1,0},{2,3},{3,2},{4,5},{5,4},{6,7},{7,6},{8,9},{9,8},{10,11... | collective-permute-start | bytes 98312 | tf_op jit(solution)/shard_map/ppermute | solution.py:93
  53.9 3.7 %collective-permute-start.11 = (f32[8,1024]{1,0:T(8,128)S(1)}, f32[8,1024]{1,0:T(8,128)S(1)}, u32[]{:S(2)}, u32[]{:S(2)}) collective-permute-start(f32[8,1024]{1,0:T(8,128)S(1)} %get-tuple-element.96.refs_0_), channel_id=1, source_target_pairs={{0,1},{1,0},{2,3},{3,2},{4,5},{5,4},{6,7},{7,6},{8,9},{9,8},{10,11... | collective-permute-start | bytes 98312 | tf_op jit(solution)/shard_map/ppermute | solution.py:93
  57.7 7.9 %collective-permute-start.14 = (f32[8,1024]{1,0:T(8,128)S(1)}, f32[8,1024]{1,0:T(8,128)S(1)}, u32[]{:S(2)}, u32[]{:S(2)}) collective-permute-start(f32[8,1024]{1,0:T(8,128)S(1)} %chip_sum.3.refs_2_.refs_3_), channel_id=1, source_target_pairs={{0,5},{1,7},{2,3},{3,9},{4,1},{5,11},{6,0},{7,13},{8,2},{9,15},{10... | collective-permute-start | bytes 98312 | tf_op jit(solution)/shard_map/ppermute | solution.py:112
  59.3 7.9 %collective-permute-start.13 = (f32[8,1024]{1,0:T(8,128)S(1)}, f32[8,1024]{1,0:T(8,128)S(1)}, u32[]{:S(2)}, u32[]{:S(2)}) collective-permute-start(f32[8,1024]{1,0:T(8,128)S(1)} %chip_sum.3.refs_2_.refs_3_), channel_id=1, source_target_pairs={{0,3},{1,5},{2,1},{3,7},{4,0},{5,9},{6,2},{7,11},{8,4},{9,13},{10,... | collective-permute-start | bytes 98312 | tf_op jit(solution)/shard_map/ppermute | solution.py:112
  62.8 4.4 %collective-permute-start.12 = (f32[8,1024]{1,0:T(8,128)S(1)}, f32[8,1024]{1,0:T(8,128)S(1)}, u32[]{:S(2)}, u32[]{:S(2)}) collective-permute-start(f32[8,1024]{1,0:T(8,128)S(1)} %chip_sum.3.refs_2_.refs_3_), channel_id=1, source_target_pairs={{0,1},{1,3},{2,0},{3,5},{4,2},{5,7},{6,4},{7,9},{8,6},{9,11},{10,8... | collective-permute-start | bytes 98312 | tf_op jit(solution)/shard_map/ppermute | solution.py:112
  67.2 6.6 %collective-permute-start.15 = (f32[8,1024]{1,0:T(8,128)S(1)}, f32[8,1024]{1,0:T(8,128)S(1)}, u32[]{:S(2)}, u32[]{:S(2)}) collective-permute-start(f32[8,1024]{1,0:T(8,128)S(1)} %near_sum.3.refs_3_.refs_4_), channel_id=1, source_target_pairs={{0,1},{1,0},{2,3},{3,2},{4,5},{5,4},{6,7},{7,6},{8,9},{9,8},{10,11... | collective-permute-start | bytes 98312 | tf_op jit(solution)/shard_map/ppermute | solution.py:93
  71.3 4.3 %collective-permute-start.16 = (f32[128,1024]{1,0:T(8,128)S(1)}, f32[128,1024]{1,0:T(8,128)S(1)}, u32[]{:S(2)}, u32[]{:S(2)}) collective-permute-start(f32[128,1024]{1,0:T(8,128)S(1)} %get-tuple-element.101), channel_id=1, source_target_pairs={{0,1},{1,0},{2,3},{3,2},{4,5},{5,4},{6,7},{7,6},{8,9},{9,8},{10,11... | collective-permute-start | bytes 1572872 | tf_op jit(solution)/shard_map/ppermute | solution.py:93
  71.4 12.9 %collective-permute-start.18 = (f32[128,1024]{1,0:T(8,128)S(1)}, f32[128,1024]{1,0:T(8,128)S(1)}, u32[]{:S(2)}, u32[]{:S(2)}) collective-permute-start(f32[128,1024]{1,0:T(8,128)S(1)} %get-tuple-element.104), channel_id=1, source_target_pairs={{0,127},{1,2},{2,1},{3,4},{4,3},{5,6},{6,5},{7,8},{8,7},{9,10},{10... | collective-permute-start | bytes 1572872 | tf_op jit(solution)/shard_map/ppermute | solution.py:99
  73.8 10.5 %collective-permute-start.17 = (f32[128,1024]{1,0:T(8,128)S(1)}, f32[128,1024]{1,0:T(8,128)S(1)}, u32[]{:S(2)}, u32[]{:S(2)}) collective-permute-start(f32[128,1024]{1,0:T(8,128)S(1)} %get-tuple-element.103), channel_id=1, source_target_pairs={{0,1},{1,0},{2,3},{3,2},{4,5},{5,4},{6,7},{7,6},{8,9},{9,8},{10,11... | collective-permute-start | bytes 1572872 | tf_op jit(solution)/shard_map/ppermute | solution.py:93
  74.0 13.2 %collective-permute-start.19 = (f32[128,1024]{1,0:T(8,128)S(1)}, f32[128,1024]{1,0:T(8,128)S(1)}, u32[]{:S(2)}, u32[]{:S(2)}) collective-permute-start(f32[128,1024]{1,0:T(8,128)S(1)} %get-tuple-element.126), channel_id=1, source_target_pairs={{0,1},{1,0},{2,3},{3,2},{4,5},{5,4},{6,7},{7,6},{8,9},{9,8},{10,11... | collective-permute-start | bytes 1572872 | tf_op jit(solution)/shard_map/ppermute | solution.py:93
  75.6 12.6 %collective-permute-start.20 = (f32[128,1024]{1,0:T(8,128)S(1)}, f32[128,1024]{1,0:T(8,128)S(1)}, u32[]{:S(2)}, u32[]{:S(2)}) collective-permute-start(f32[128,1024]{1,0:T(8,128)S(1)} %get-tuple-element.128), channel_id=1, source_target_pairs={{0,1},{1,3},{2,0},{3,5},{4,2},{5,7},{6,4},{7,9},{8,6},{9,11},{10,8... | collective-permute-start | bytes 1572872 | tf_op jit(solution)/shard_map/ppermute | solution.py:112
  84.4 13.5 %collective-permute-start.21 = (f32[128,1024]{1,0:T(8,128)S(1)}, f32[128,1024]{1,0:T(8,128)S(1)}, u32[]{:S(2)}, u32[]{:S(2)}) collective-permute-start(f32[128,1024]{1,0:T(8,128)S(1)} %get-tuple-element.129), channel_id=1, source_target_pairs={{0,2},{1,0},{2,4},{3,1},{4,6},{5,3},{6,8},{7,5},{8,10},{9,7},{10,1... | collective-permute-start | bytes 1572872 | tf_op jit(solution)/shard_map/ppermute | solution.py:112

commit v3 on v2

--- a/solution.py
+++ b/solution.py
@@ -17,7 +17,7 @@
 OFFSETS = (0, 1, 2, -2, -3, -1, 3)
 SLOT = {offset: slot for slot, offset in enumerate(OFFSETS)}
 SLOTS = 7
-RELAYED = (2, 3)
+RELAYED = ()
 SCALE = 10.0 * math.log2(math.e)
 F32 = jnp.float32
 BF16 = jnp.bfloat16
@@ -415,10 +415,11 @@
 
     kernel_block(0, slab)
     kernel_block(1, other)
-    shared_two = partner(kernel_block(3, behind_one))
-    relayed = kernel_block(2, ahead_one)
-    third = beside(relayed)
-    shared = partner(relayed)
+    third = beside(ahead_one)
+    shared_two = partner(behind_one)
+    shared = partner(ahead_one)
+    kernel_block(3, behind_one)
+    kernel_block(2, ahead_one)
     kernel_block(6, shared_two)
     kernel_block(5, shared)
     kernel_block(4, third)

time: 101 us -> 98.2 us (0.972)
  the two profiles are of different devices: /device:TPU:16 before, /device:TPU:25 now
where the time goes in v3:
time: 98.2 us; the launch traced here: 99.2 us
  Pallas kernels  39.5 us (40%)
  starting transfers between devices  36 us (37%)
  waiting for transfers between devices  21.4 us (22%)
  between operations  1.62 us (2%)
    pallas_call x31, Pallas kernels, local(): pl.pallas_call(with_tokens, out_shape=outs, in_specs=[SMEM] * scalars + [...  39.5 us
    ppermute x10, starting transfers between devices, relayed(): return lax.ppermute(block, 'dev', route)  17.9 us
    ppermute x10, starting transfers between devices, partner(): lax.ppermute(block, 'dev', [(i, i + 1 - 2 * (i % 2)) for i in range(devic...  17.6 us
    ppermute x10, waiting for transfers between devices, relayed(): return lax.ppermute(block, 'dev', route)  14.7 us
    ppermute x2, waiting for transfers between devices, beside(): return lax.ppermute(block, 'dev', route)  3.4 us
    ppermute x10, waiting for transfers between devices, partner(): lax.ppermute(block, 'dev', [(i, i + 1 - 2 * (i % 2)) for i in range(devic...  3.27 us
  transfers between devices with their start and end apart: 22, of which 11 were waited for; matrix products, arithmetic and copies ran while one was open for 0% of the time, Pallas kernels for 29%

profile of v3, /device:TPU:25, one launch (start us, length us, event | category | flops | bytes accessed | tf_op | source)
XLA Modules:
  0.0 99.2 jit_solution(17292978859010796519)
XLA Ops:
  0.6 1.3 %slab.1.refs_5_.refs_2_ = f32[136,1024]{1,0:T(8,128)S(1)} custom-call(f32[1024,128]{1,0:T(8,128)} %refs_0_.2, s32[1,1024]{1,0:T(1,128)} %bitcast.4, f32[1,1024]{1,0:T(1,128)} %bitcast.5), custom_call_target="tpu_custom_call" | custom-call | flops 1000000000 | bytes 3000000 | tf_op jit(solution)/shard_map/slab/pallas_call | solution.py:76
  1.9 1.7 %collective-permute-start = (f32[136,1024]{1,0:T(8,128)S(1)}, f32[136,1024]{1,0:T(8,128)S(1)}, u32[]{:S(2)}, u32[]{:S(2)}) collective-permute-start(f32[136,1024]{1,0:T(8,128)S(1)} %slab.1.refs_5_.refs_2_), channel_id=1, source_target_pairs={{0,1},{1,3},{2,0},{3,5},{4,2},{5,7},{6,4},{7,9},{8,6},{9,11},{10,8... | collective-permute-start | bytes 1671176 | tf_op jit(solution)/shard_map/ppermute | solution.py:112
  3.6 4.6 %collective-permute-start.3 = (f32[136,1024]{1,0:T(8,128)S(1)}, f32[136,1024]{1,0:T(8,128)S(1)}, u32[]{:S(2)}, u32[]{:S(2)}) collective-permute-start(f32[136,1024]{1,0:T(8,128)S(1)} %slab.1.refs_5_.refs_2_), channel_id=1, source_target_pairs={{0,2},{1,0},{2,4},{3,1},{4,6},{5,3},{6,8},{7,5},{8,10},{9,7},{10,1... | collective-permute-start | bytes 1671176 | tf_op jit(solution)/shard_map/ppermute | solution.py:112
  10.4 2.1 %left.1 = (bf16[1024,512]{1,0:T(8,128)(2,1)S(1)}, f32[1024,128]{1,0:T(8,128)S(1)}, s32[8]{0:T(128)S(4)}) custom-call(s32[1,7]{1,0:T(1,128)S(1)} %copy-done.1, s32[1]{0:T(128)S(6)} %copy.86.refs_1_, f32[1024,128]{1,0:T(8,128)} %refs_1_.2, s32[1,1024]{1,0:T(1,128)} %bitcast.6, f32[1,1024]{1,0:T(1,128)} %bitcast.7, f32[136,1024]{1,0:T(8,128)S(1)} %slab.1.refs_5_.refs_2_), custom_call_target="tpu_custom_call" | custom-call | flops 1000000000 | bytes 3000000 | tf_op jit(solution)/shard_map/left/pallas_call | solution.py:76
  12.5 1.3 %kernel_block.7 = (f32[7,1024,1024]{2,1,0:T(8,128)S(1)}, f32[1024,128]{1,0:T(8,128)S(1)}, f32[8,1024]{1,0:T(8,128)S(1)}) custom-call(s32[8]{0:T(128)S(4)} %get-tuple-element.64.refs_0_, bf16[1024,512]{1,0:T(8,128)(2,1)S(1)} %get-tuple-element.65.refs_1_, f32[136,1024]{1,0:T(8,128)S(1)} %slab.1.refs_5_.refs_2_), custom_call_target="tpu_custom_call" | custom-call | flops 2000000000 | bytes 6000000 | tf_op jit(solution)/shard_map/kernel_block/pallas_call | solution.py:76
  15.0 6.0 %collective-permute-start.2 = (f32[136,1024]{1,0:T(8,128)S(1)}, f32[136,1024]{1,0:T(8,128)S(1)}, u32[]{:S(2)}, u32[]{:S(2)}) collective-permute-start(f32[136,1024]{1,0:T(8,128)S(1)} %collective-permute-done.refs_2_), channel_id=1, source_target_pairs={{0,1},{1,0},{2,3},{3,2},{4,5},{5,4},{6,7},{7,6},{8,9},{9,8},{10,11... | collective-permute-start | bytes 1671176 | tf_op jit(solution)/shard_map/ppermute | solution.py:93
  21.0 6.8 %collective-permute-start.4 = (f32[136,1024]{1,0:T(8,128)S(1)}, f32[136,1024]{1,0:T(8,128)S(1)}, u32[]{:S(2)}, u32[]{:S(2)}) collective-permute-start(f32[136,1024]{1,0:T(8,128)S(1)} %collective-permute-done.3.refs_2_), channel_id=1, source_target_pairs={{0,1},{1,0},{2,3},{3,2},{4,5},{5,4},{6,7},{7,6},{8,9},{9,8},{10,11... | collective-permute-start | bytes 1671176 | tf_op jit(solution)/shard_map/ppermute | solution.py:93
  27.9 1.3 %kernel_block.8 = (f32[7,1024,1024]{2,1,0:T(8,128)S(1)}, f32[1024,128]{1,0:T(8,128)S(1)}, f32[8,1024]{1,0:T(8,128)S(1)}) custom-call(s32[8]{0:T(128)S(4)} %get-tuple-element.64.refs_0_, bf16[1024,512]{1,0:T(8,128)(2,1)S(1)} %get-tuple-element.65.refs_1_, ...), custom_call_target="tpu_custom_call", output_to_operand_aliasing={{0}: (3, {}), {1}: (4, {})} | custom-call | flops 2000000000 | bytes 6000000 | tf_op jit(solution)/shard_map/kernel_block/pallas_call | solution.py:76
  29.2 1.4 %kernel_block.9 = (f32[7,1024,1024]{2,1,0:T(8,128)S(1)}, f32[1024,128]{1,0:T(8,128)S(1)}, f32[8,1024]{1,0:T(8,128)S(1)}) custom-call(s32[8]{0:T(128)S(4)} %get-tuple-element.64.refs_0_, bf16[1024,512]{1,0:T(8,128)(2,1)S(1)} %get-tuple-element.65.refs_1_, ...), custom_call_target="tpu_custom_call", output_to_operand_aliasing={{0}: (3, {}), {1}: (4, {})} | custom-call | flops 2000000000 | bytes 6000000 | tf_op jit(solution)/shard_map/kernel_block/pallas_call | solution.py:76
  30.6 1.4 %kernel_block.10 = (f32[7,1024,1024]{2,1,0:T(8,128)S(1)}, f32[1024,128]{1,0:T(8,128)S(1)}, f32[8,1024]{1,0:T(8,128)S(1)}) custom-call(s32[8]{0:T(128)S(4)} %get-tuple-element.64.refs_0_, bf16[1024,512]{1,0:T(8,128)(2,1)S(1)} %get-tuple-element.65.refs_1_, ...), custom_call_target="tpu_custom_call", output_to_operand_aliasing={{0}: (3, {}), {1}: (4, {})} | custom-call | flops 2000000000 | bytes 6000000 | tf_op jit(solution)/shard_map/kernel_block/pallas_call | solution.py:76
  31.9 1.4 %kernel_block.11 = (f32[7,1024,1024]{2,1,0:T(8,128)S(1)}, f32[1024,128]{1,0:T(8,128)S(1)}, f32[8,1024]{1,0:T(8,128)S(1)}) custom-call(s32[8]{0:T(128)S(4)} %get-tuple-element.64.refs_0_, bf16[1024,512]{1,0:T(8,128)(2,1)S(1)} %get-tuple-element.65.refs_1_, ...), custom_call_target="tpu_custom_call", output_to_operand_aliasing={{0}: (3, {}), {1}: (4, {})} | custom-call | flops 2000000000 | bytes 6000000 | tf_op jit(solution)/shard_map/kernel_block/pallas_call | solution.py:76
  33.3 1.4 %kernel_block.12 = (f32[7,1024,1024]{2,1,0:T(8,128)S(1)}, f32[1024,128]{1,0:T(8,128)S(1)}, f32[8,1024]{1,0:T(8,128)S(1)}) custom-call(s32[8]{0:T(128)S(4)} %get-tuple-element.64.refs_0_, bf16[1024,512]{1,0:T(8,128)(2,1)S(1)} %get-tuple-element.65.refs_1_, ...), custom_call_target="tpu_custom_call", output_to_operand_aliasing={{0}: (3, {}), {1}: (4, {})} | custom-call | flops 2000000000 | bytes 6000000 | tf_op jit(solution)/shard_map/kernel_block/pallas_call | solution.py:76
  34.7 1.4 %kernel_block.13 = (f32[7,1024,1024]{2,1,0:T(8,128)S(1)}, f32[1024,128]{1,0:T(8,128)S(1)}, f32[8,1024]{1,0:T(8,128)S(1)}) custom-call(s32[8]{0:T(128)S(4)} %get-tuple-element.64.refs_0_, bf16[1024,512]{1,0:T(8,128)(2,1)S(1)} %get-tuple-element.65.refs_1_, ...), custom_call_target="tpu_custom_call", output_to_operand_aliasing={{0}: (3, {}), {1}: (4, {})} | custom-call | flops 2000000000 | bytes 6000000 | tf_op jit(solution)/shard_map/kernel_block/pallas_call | solution.py:76
  36.1 2.5 %first_scales.1 = (f32[7,1024,1024]{2,1,0:T(8,128)S(1)}, f32[8,1024]{1,0:T(8,128)S(1)}) custom-call(s32[8]{0:T(128)S(4)} %get-tuple-element.64.refs_0_, f32[7,1024,1024]{2,1,0:T(8,128)S(1)} %get-tuple-element.78.refs_1_, f32[1024,128]{1,0:T(8,128)S(1)} %get-tuple-element.79.refs_2_, ...), custom_call_target="tpu_custom_call", output_to_operand_aliasing={{0}: (1, {})} | custom-call | flops 3000000000 | bytes 9000000 | tf_op jit(solution)/shard_map/first_scales/pallas_call | solution.py:76
  40.3 5.6 %collective-permute-done.9.refs_2_ = f32[8,1024]{1,0:T(8,128)S(1)} collective-permute-done((f32[8,1024]{1,0:T(8,128)S(1)}, f32[8,1024]{1,0:T(8,128)S(1)}, u32[]{:S(2)}, u32[]{:S(2)}) %collective-permute-start.9) | collective-permute-done | bytes 32800 | tf_op jit(solution)/shard_map/ppermute | solution.py:112
  45.9 1.6 %collective-permute-done.8.refs_1_ = f32[8,1024]{1,0:T(8,128)S(1)} collective-permute-done((f32[8,1024]{1,0:T(8,128)S(1)}, f32[8,1024]{1,0:T(8,128)S(1)}, u32[]{:S(2)}, u32[]{:S(2)}) %collective-permute-start.8) | collective-permute-done | bytes 32800 | tf_op jit(solution)/shard_map/ppermute | solution.py:112
  48.1 1.9 %collective-permute-start.10 = (f32[8,1024]{1,0:T(8,128)S(1)}, f32[8,1024]{1,0:T(8,128)S(1)}, u32[]{:S(2)}, u32[]{:S(2)}) collective-permute-start(f32[8,1024]{1,0:T(8,128)S(1)} %near_sum.2.refs_3_), channel_id=1, source_target_pairs={{0,1},{1,0},{2,3},{3,2},{4,5},{5,4},{6,7},{7,6},{8,9},{9,8},{10,11... | collective-permute-start | bytes 98312 | tf_op jit(solution)/shard_map/ppermute | solution.py:93
  50.8 4.9 %second_scales.1 = (f32[7,1024,1024]{2,1,0:T(8,128)S(1)}, f32[1024,128]{1,0:T(8,128)S(1)}, f32[8,1024]{1,0:T(8,128)S(1)}) custom-call(s32[8]{0:T(128)S(4)} %get-tuple-element.64.refs_0_, f32[7,1024,1024]{2,1,0:T(8,128)S(1)} %get-tuple-element.81.refs_1_, f32[8,1024]{1,0:T(8,128)S(1)} %chip_sum.2.refs_2_, ...), custom_call_target="tpu_custom_call", output_to_operand_aliasing={{0}: (1, {})} | custom-call | flops 5000000000 | bytes 15000000 | tf_op jit(solution)/shard_map/second_scales/pallas_call | solution.py:76
  57.0 3.0 %collective-permute-start.14 = (f32[8,1024]{1,0:T(8,128)S(1)}, f32[8,1024]{1,0:T(8,128)S(1)}, u32[]{:S(2)}, u32[]{:S(2)}) collective-permute-start(f32[8,1024]{1,0:T(8,128)S(1)} %chip_sum.3.refs_2_.refs_3_), channel_id=1, source_target_pairs={{0,5},{1,7},{2,3},{3,9},{4,1},{5,11},{6,0},{7,13},{8,2},{9,15},{10... | collective-permute-start | bytes 98312 | tf_op jit(solution)/shard_map/ppermute | solution.py:112
  60.0 1.3 %collective-permute-start.13 = (f32[8,1024]{1,0:T(8,128)S(1)}, f32[8,1024]{1,0:T(8,128)S(1)}, u32[]{:S(2)}, u32[]{:S(2)}) collective-permute-start(f32[8,1024]{1,0:T(8,128)S(1)} %chip_sum.3.refs_2_.refs_3_), channel_id=1, source_target_pairs={{0,3},{1,5},{2,1},{3,7},{4,0},{5,9},{6,2},{7,11},{8,4},{9,13},{10,... | collective-permute-start | bytes 98312 | tf_op jit(solution)/shard_map/ppermute | solution.py:112
  63.0 4.3 %collective-permute-done.13.refs_1_ = f32[8,1024]{1,0:T(8,128)S(1)} collective-permute-done((f32[8,1024]{1,0:T(8,128)S(1)}, f32[8,1024]{1,0:T(8,128)S(1)}, u32[]{:S(2)}, u32[]{:S(2)}) %collective-permute-start.13) | collective-permute-done | bytes 32800 | tf_op jit(solution)/shard_map/ppermute | solution.py:112
  67.3 1.3 %collective-permute-done.12.refs_0_ = f32[8,1024]{1,0:T(8,128)S(1)} collective-permute-done((f32[8,1024]{1,0:T(8,128)S(1)}, f32[8,1024]{1,0:T(8,128)S(1)}, u32[]{:S(2)}, u32[]{:S(2)}) %collective-permute-start.12) | collective-permute-done | bytes 32800 | tf_op jit(solution)/shard_map/ppermute | solution.py:112
  71.5 1.6 %collective-permute-start.17 = (f32[128,1024]{1,0:T(8,128)S(1)}, f32[128,1024]{1,0:T(8,128)S(1)}, u32[]{:S(2)}, u32[]{:S(2)}) collective-permute-start(f32[128,1024]{1,0:T(8,128)S(1)} %get-tuple-element.99), channel_id=1, source_target_pairs={{0,1},{1,0},{2,3},{3,2},{4,5},{5,4},{6,7},{7,6},{8,9},{9,8},{10,11... | collective-permute-start | bytes 1572872 | tf_op jit(solution)/shard_map/ppermute | solution.py:93
  75.4 3.4 %collective-permute-done.18.refs_4_ = f32[128,1024]{1,0:T(8,128)S(1)} collective-permute-done((f32[128,1024]{1,0:T(8,128)S(1)}, f32[128,1024]{1,0:T(8,128)S(1)}, u32[]{:S(2)}, u32[]{:S(2)}) %collective-permute-start.18) | collective-permute-done | bytes 524320 | tf_op jit(solution)/shard_map/ppermute | solution.py:99
  79.9 6.6 %collective-permute-start.21 = (f32[128,1024]{1,0:T(8,128)S(1)}, f32[128,1024]{1,0:T(8,128)S(1)}, u32[]{:S(2)}, u32[]{:S(2)}) collective-permute-start(f32[128,1024]{1,0:T(8,128)S(1)} %get-tuple-element.125), channel_id=1, source_target_pairs={{0,2},{1,0},{2,4},{3,1},{4,6},{5,3},{6,8},{7,5},{8,10},{9,7},{10,1... | collective-permute-start | bytes 1572872 | tf_op jit(solution)/shard_map/ppermute | solution.py:112
  86.5 1.3 %ahead_map.7 = (f32[7,1024,1024]{2,1,0:T(8,128)S(1)}, f32[1024,128]{1,0:T(8,128)S(1)}, f32[1024,128]{1,0:T(8,128)S(1)}) custom-call(s32[8]{0:T(128)S(4)} %get-tuple-element.64.refs_0_, f32[7,1024,1024]{2,1,0:T(8,128)S(1)} %get-tuple-element.101.refs_1_, f32[136,1024]{1,0:T(8,128)S(1)} %slab.1.refs_5_.refs_2_, ...), custom_call_target="tpu_custom_call", output_to_operand_aliasing={{0}: (1, {})} | custom-call | flops 2000000000 | bytes 6000000 | tf_op jit(solution)/shard_map/ahead_map/pallas_call | solution.py:76
  87.9 1.4 %ahead_map.8 = (f32[7,1024,1024]{2,1,0:T(8,128)S(1)}, f32[1024,128]{1,0:T(8,128)S(1)}, f32[1024,128]{1,0:T(8,128)S(1)}) custom-call(s32[8]{0:T(128)S(4)} %get-tuple-element.64.refs_0_, f32[7,1024,1024]{2,1,0:T(8,128)S(1)} %get-tuple-element.102.refs_1_, ...), custom_call_target="tpu_custom_call", output_to_operand_aliasing={{0}: (1, {}), {1}: (7, {}), {2}: (8, {})} | custom-call | flops 2000000000 | bytes 6000000 | tf_op jit(solution)/shard_map/ahead_map/pallas_call | solution.py:76
  89.2 1.4 %ahead_map.9 = (f32[7,1024,1024]{2,1,0:T(8,128)S(1)}, f32[1024,128]{1,0:T(8,128)S(1)}, f32[1024,128]{1,0:T(8,128)S(1)}) custom-call(s32[8]{0:T(128)S(4)} %get-tuple-element.64.refs_0_, f32[7,1024,1024]{2,1,0:T(8,128)S(1)} %get-tuple-element.105.refs_1_, ...), custom_call_target="tpu_custom_call", output_to_operand_aliasing={{0}: (1, {}), {1}: (7, {}), {2}: (8, {})} | custom-call | flops 2000000000 | bytes 6000000 | tf_op jit(solution)/shard_map/ahead_map/pallas_call | solution.py:76
  90.6 1.4 %ahead_map.10 = (f32[7,1024,1024]{2,1,0:T(8,128)S(1)}, f32[1024,128]{1,0:T(8,128)S(1)}, f32[1024,128]{1,0:T(8,128)S(1)}) custom-call(s32[8]{0:T(128)S(4)} %get-tuple-element.64.refs_0_, f32[7,1024,1024]{2,1,0:T(8,128)S(1)} %get-tuple-element.108.refs_1_, ...), custom_call_target="tpu_custom_call", output_to_operand_aliasing={{0}: (1, {}), {1}: (7, {}), {2}: (8, {})} | custom-call | flops 2000000000 | bytes 6000000 | tf_op jit(solution)/shard_map/ahead_map/pallas_call | solution.py:76
  92.0 1.4 %ahead_map.11 = (f32[7,1024,1024]{2,1,0:T(8,128)S(1)}, f32[1024,128]{1,0:T(8,128)S(1)}, f32[1024,128]{1,0:T(8,128)S(1)}) custom-call(s32[8]{0:T(128)S(4)} %get-tuple-element.64.refs_0_, f32[7,1024,1024]{2,1,0:T(8,128)S(1)} %get-tuple-element.111.refs_1_, ...), custom_call_target="tpu_custom_call", output_to_operand_aliasing={{0}: (1, {}), {1}: (7, {}), {2}: (8, {})} | custom-call | flops 2000000000 | bytes 6000000 | tf_op jit(solution)/shard_map/ahead_map/pallas_call | solution.py:76
  93.4 1.4 %ahead_map.12 = (f32[7,1024,1024]{2,1,0:T(8,128)S(1)}, f32[1024,128]{1,0:T(8,128)S(1)}, f32[1024,128]{1,0:T(8,128)S(1)}) custom-call(s32[8]{0:T(128)S(4)} %get-tuple-element.64.refs_0_, f32[7,1024,1024]{2,1,0:T(8,128)S(1)} %get-tuple-element.114.refs_1_, ...), custom_call_target="tpu_custom_call", output_to_operand_aliasing={{0}: (1, {}), {1}: (7, {}), {2}: (8, {})} | custom-call | flops 2000000000 | bytes 6000000 | tf_op jit(solution)/shard_map/ahead_map/pallas_call | solution.py:76
  94.7 2.4 %ahead_map.13 = (f32[7,1024,1024]{2,1,0:T(8,128)S(1)}, f32[1024,128]{1,0:T(8,128)}) custom-call(s32[8]{0:T(128)S(4)} %get-tuple-element.64.refs_0_, f32[7,1024,1024]{2,1,0:T(8,128)S(1)} %get-tuple-element.117.refs_1_, f32[136,1024]{1,0:T(8,128)S(1)} %collective-permute-done.4.refs_2_, ...), custom_call_target="tpu_custom_call", output_to_operand_aliasing={{0}: (1, {})} | custom-call | flops 2000000000 | bytes 6000000 | tf_op jit(solution)/shard_map/ahead_map/pallas_call | solution.py:76
  (47 shorter events, 17.2 us)
Async XLA Ops:
  1.9 13.1 %collective-permute-start = (f32[136,1024]{1,0:T(8,128)S(1)}, f32[136,1024]{1,0:T(8,128)S(1)}, u32[]{:S(2)}, u32[]{:S(2)}) collective-permute-start(f32[136,1024]{1,0:T(8,128)S(1)} %slab.1.refs_5_.refs_2_), channel_id=1, source_target_pairs={{0,1},{1,3},{2,0},{3,5},{4,2},{5,7},{6,4},{7,9},{8,6},{9,11},{10,8... | collective-permute-start | bytes 1671176 | tf_op jit(solution)/shard_map/ppermute | solution.py:112
  3.6 17.4 %collective-permute-start.3 = (f32[136,1024]{1,0:T(8,128)S(1)}, f32[136,1024]{1,0:T(8,128)S(1)}, u32[]{:S(2)}, u32[]{:S(2)}) collective-permute-start(f32[136,1024]{1,0:T(8,128)S(1)} %slab.1.refs_5_.refs_2_), channel_id=1, source_target_pairs={{0,2},{1,0},{2,4},{3,1},{4,6},{5,3},{6,8},{7,5},{8,10},{9,7},{10,1... | collective-permute-start | bytes 1671176 | tf_op jit(solution)/shard_map/ppermute | solution.py:112
  8.2 19.7 %collective-permute-start.5 = (f32[136,1024]{1,0:T(8,128)S(1)}, f32[136,1024]{1,0:T(8,128)S(1)}, u32[]{:S(2)}, u32[]{:S(2)}) collective-permute-start(f32[136,1024]{1,0:T(8,128)S(1)} %slab.1.refs_5_.refs_2_), channel_id=1, source_target_pairs={{0,1},{1,0},{2,3},{3,2},{4,5},{5,4},{6,7},{7,6},{8,9},{9,8},{10,11... | collective-permute-start | bytes 1671176 | tf_op jit(solution)/shard_map/ppermute | solution.py:93
  9.7 0.7 copy-start.1
  15.0 18.3 %collective-permute-start.2 = (f32[136,1024]{1,0:T(8,128)S(1)}, f32[136,1024]{1,0:T(8,128)S(1)}, u32[]{:S(2)}, u32[]{:S(2)}) collective-permute-start(f32[136,1024]{1,0:T(8,128)S(1)} %collective-permute-done.refs_2_), channel_id=1, source_target_pairs={{0,1},{1,0},{2,3},{3,2},{4,5},{5,4},{6,7},{7,6},{8,9},{9,8},{10,11... | collective-permute-start | bytes 1671176 | tf_op jit(solution)/shard_map/ppermute | solution.py:93
  21.0 13.6 %collective-permute-start.1 = (f32[136,1024]{1,0:T(8,128)S(1)}, f32[136,1024]{1,0:T(8,128)S(1)}, u32[]{:S(2)}, u32[]{:S(2)}) collective-permute-start(f32[136,1024]{1,0:T(8,128)S(1)} %collective-permute-done.refs_2_), channel_id=1, source_target_pairs={{0,127},{1,2},{2,1},{3,4},{4,3},{5,6},{6,5},{7,8},{8,7},{9,10},{10... | collective-permute-start | bytes 1671176 | tf_op jit(solution)/shard_map/ppermute | solution.py:99
  21.0 10.9 %collective-permute-start.4 = (f32[136,1024]{1,0:T(8,128)S(1)}, f32[136,1024]{1,0:T(8,128)S(1)}, u32[]{:S(2)}, u32[]{:S(2)}) collective-permute-start(f32[136,1024]{1,0:T(8,128)S(1)} %collective-permute-done.3.refs_2_), channel_id=1, source_target_pairs={{0,1},{1,0},{2,3},{3,2},{4,5},{5,4},{6,7},{7,6},{8,9},{9,8},{10,11... | collective-permute-start | bytes 1671176 | tf_op jit(solution)/shard_map/ppermute | solution.py:93
  36.0 25.4 %copy-start = (f32[1024,128]{1,0:T(8,128)S(1)}, f32[1024,128]{1,0:T(8,128)}, u32[]{:S(2)}) copy-start(f32[1024,128]{1,0:T(8,128)} %refs_1_.2) | copy-start | bytes 1572868
  38.5 1.3 %collective-permute-start.6 = (f32[8,1024]{1,0:T(8,128)S(1)}, f32[8,1024]{1,0:T(8,128)S(1)}, u32[]{:S(2)}, u32[]{:S(2)}) collective-permute-start(f32[8,1024]{1,0:T(8,128)S(1)} %get-tuple-element.82.refs_0_), channel_id=1, source_target_pairs={{0,1},{1,0},{2,3},{3,2},{4,5},{5,4},{6,7},{7,6},{8,9},{9,8},{10,11... | collective-permute-start | bytes 98312 | tf_op jit(solution)/shard_map/ppermute | solution.py:93
  39.8 6.0 %collective-permute-start.9 = (f32[8,1024]{1,0:T(8,128)S(1)}, f32[8,1024]{1,0:T(8,128)S(1)}, u32[]{:S(2)}, u32[]{:S(2)}) collective-permute-start(f32[8,1024]{1,0:T(8,128)S(1)} %chip_sum.2.refs_2_), channel_id=1, source_target_pairs={{0,5},{1,7},{2,3},{3,9},{4,1},{5,11},{6,0},{7,13},{8,2},{9,15},{10... | collective-permute-start | bytes 98312 | tf_op jit(solution)/shard_map/ppermute | solution.py:112
  40.1 7.3 %collective-permute-start.8 = (f32[8,1024]{1,0:T(8,128)S(1)}, f32[8,1024]{1,0:T(8,128)S(1)}, u32[]{:S(2)}, u32[]{:S(2)}) collective-permute-start(f32[8,1024]{1,0:T(8,128)S(1)} %chip_sum.2.refs_2_), channel_id=1, source_target_pairs={{0,3},{1,5},{2,1},{3,7},{4,0},{5,9},{6,2},{7,11},{8,4},{9,13},{10,... | collective-permute-start | bytes 98312 | tf_op jit(solution)/shard_map/ppermute | solution.py:112
  40.2 7.9 %collective-permute-start.7 = (f32[8,1024]{1,0:T(8,128)S(1)}, f32[8,1024]{1,0:T(8,128)S(1)}, u32[]{:S(2)}, u32[]{:S(2)}) collective-permute-start(f32[8,1024]{1,0:T(8,128)S(1)} %chip_sum.2.refs_2_), channel_id=1, source_target_pairs={{0,1},{1,3},{2,0},{3,5},{4,2},{5,7},{6,4},{7,9},{8,6},{9,11},{10,8... | collective-permute-start | bytes 98312 | tf_op jit(solution)/shard_map/ppermute | solution.py:112
  48.1 2.7 %collective-permute-start.10 = (f32[8,1024]{1,0:T(8,128)S(1)}, f32[8,1024]{1,0:T(8,128)S(1)}, u32[]{:S(2)}, u32[]{:S(2)}) collective-permute-start(f32[8,1024]{1,0:T(8,128)S(1)} %near_sum.2.refs_3_), channel_id=1, source_target_pairs={{0,1},{1,0},{2,3},{3,2},{4,5},{5,4},{6,7},{7,6},{8,9},{9,8},{10,11... | collective-permute-start | bytes 98312 | tf_op jit(solution)/shard_map/ppermute | solution.py:93
  55.7 1.3 %collective-permute-start.11 = (f32[8,1024]{1,0:T(8,128)S(1)}, f32[8,1024]{1,0:T(8,128)S(1)}, u32[]{:S(2)}, u32[]{:S(2)}) collective-permute-start(f32[8,1024]{1,0:T(8,128)S(1)} %get-tuple-element.92.refs_0_), channel_id=1, source_target_pairs={{0,1},{1,0},{2,3},{3,2},{4,5},{5,4},{6,7},{7,6},{8,9},{9,8},{10,11... | collective-permute-start | bytes 98312 | tf_op jit(solution)/shard_map/ppermute | solution.py:93
  57.0 5.9 %collective-permute-start.14 = (f32[8,1024]{1,0:T(8,128)S(1)}, f32[8,1024]{1,0:T(8,128)S(1)}, u32[]{:S(2)}, u32[]{:S(2)}) collective-permute-start(f32[8,1024]{1,0:T(8,128)S(1)} %chip_sum.3.refs_2_.refs_3_), channel_id=1, source_target_pairs={{0,5},{1,7},{2,3},{3,9},{4,1},{5,11},{6,0},{7,13},{8,2},{9,15},{10... | collective-permute-start | bytes 98312 | tf_op jit(solution)/shard_map/ppermute | solution.py:112
  60.0 7.3 %collective-permute-start.13 = (f32[8,1024]{1,0:T(8,128)S(1)}, f32[8,1024]{1,0:T(8,128)S(1)}, u32[]{:S(2)}, u32[]{:S(2)}) collective-permute-start(f32[8,1024]{1,0:T(8,128)S(1)} %chip_sum.3.refs_2_.refs_3_), channel_id=1, source_target_pairs={{0,3},{1,5},{2,1},{3,7},{4,0},{5,9},{6,2},{7,11},{8,4},{9,13},{10,... | collective-permute-start | bytes 98312 | tf_op jit(solution)/shard_map/ppermute | solution.py:112
  61.3 7.2 %collective-permute-start.12 = (f32[8,1024]{1,0:T(8,128)S(1)}, f32[8,1024]{1,0:T(8,128)S(1)}, u32[]{:S(2)}, u32[]{:S(2)}) collective-permute-start(f32[8,1024]{1,0:T(8,128)S(1)} %chip_sum.3.refs_2_.refs_3_), channel_id=1, source_target_pairs={{0,1},{1,3},{2,0},{3,5},{4,2},{5,7},{6,4},{7,9},{8,6},{9,11},{10,8... | collective-permute-start | bytes 98312 | tf_op jit(solution)/shard_map/ppermute | solution.py:112
  68.5 1.9 %collective-permute-start.15 = (f32[8,1024]{1,0:T(8,128)S(1)}, f32[8,1024]{1,0:T(8,128)S(1)}, u32[]{:S(2)}, u32[]{:S(2)}) collective-permute-start(f32[8,1024]{1,0:T(8,128)S(1)} %near_sum.3.refs_3_.refs_4_), channel_id=1, source_target_pairs={{0,1},{1,0},{2,3},{3,2},{4,5},{5,4},{6,7},{7,6},{8,9},{9,8},{10,11... | collective-permute-start | bytes 98312 | tf_op jit(solution)/shard_map/ppermute | solution.py:93
  69.7 4.5 %collective-permute-start.16 = (f32[128,1024]{1,0:T(8,128)S(1)}, f32[128,1024]{1,0:T(8,128)S(1)}, u32[]{:S(2)}, u32[]{:S(2)}) collective-permute-start(f32[128,1024]{1,0:T(8,128)S(1)} %get-tuple-element.97), channel_id=1, source_target_pairs={{0,1},{1,0},{2,3},{3,2},{4,5},{5,4},{6,7},{7,6},{8,9},{9,8},{10,11... | collective-permute-start | bytes 1572872 | tf_op jit(solution)/shard_map/ppermute | solution.py:93
  69.8 9.0 %collective-permute-start.18 = (f32[128,1024]{1,0:T(8,128)S(1)}, f32[128,1024]{1,0:T(8,128)S(1)}, u32[]{:S(2)}, u32[]{:S(2)}) collective-permute-start(f32[128,1024]{1,0:T(8,128)S(1)} %get-tuple-element.100), channel_id=1, source_target_pairs={{0,127},{1,2},{2,1},{3,4},{4,3},{5,6},{6,5},{7,8},{8,7},{9,10},{10... | collective-permute-start | bytes 1572872 | tf_op jit(solution)/shard_map/ppermute | solution.py:99
  71.5 7.3 %collective-permute-start.17 = (f32[128,1024]{1,0:T(8,128)S(1)}, f32[128,1024]{1,0:T(8,128)S(1)}, u32[]{:S(2)}, u32[]{:S(2)}) collective-permute-start(f32[128,1024]{1,0:T(8,128)S(1)} %get-tuple-element.99), channel_id=1, source_target_pairs={{0,1},{1,0},{2,3},{3,2},{4,5},{5,4},{6,7},{7,6},{8,9},{9,8},{10,11... | collective-permute-start | bytes 1572872 | tf_op jit(solution)/shard_map/ppermute | solution.py:93
  74.1 23.0 %collective-permute-start.19 = (f32[128,1024]{1,0:T(8,128)S(1)}, f32[128,1024]{1,0:T(8,128)S(1)}, u32[]{:S(2)}, u32[]{:S(2)}) collective-permute-start(f32[128,1024]{1,0:T(8,128)S(1)} %get-tuple-element.122), channel_id=1, source_target_pairs={{0,1},{1,0},{2,3},{3,2},{4,5},{5,4},{6,7},{7,6},{8,9},{9,8},{10,11... | collective-permute-start | bytes 1572872 | tf_op jit(solution)/shard_map/ppermute | solution.py:93
  75.3 22.9 %collective-permute-start.20 = (f32[128,1024]{1,0:T(8,128)S(1)}, f32[128,1024]{1,0:T(8,128)S(1)}, u32[]{:S(2)}, u32[]{:S(2)}) collective-permute-start(f32[128,1024]{1,0:T(8,128)S(1)} %get-tuple-element.124), channel_id=1, source_target_pairs={{0,1},{1,3},{2,0},{3,5},{4,2},{5,7},{6,4},{7,9},{8,6},{9,11},{10,8... | collective-permute-start | bytes 1572872 | tf_op jit(solution)/shard_map/ppermute | solution.py:112
  79.9 18.3 %collective-permute-start.21 = (f32[128,1024]{1,0:T(8,128)S(1)}, f32[128,1024]{1,0:T(8,128)S(1)}, u32[]{:S(2)}, u32[]{:S(2)}) collective-permute-start(f32[128,1024]{1,0:T(8,128)S(1)} %get-tuple-element.125), channel_id=1, source_target_pairs={{0,2},{1,0},{2,4},{3,1},{4,6},{5,3},{6,8},{7,5},{8,10},{9,7},{10,1... | collective-permute-start | bytes 1572872 | tf_op jit(solution)/shard_map/ppermute | solution.py:112
